TPU v7x, 32 devices: a whole 2x2x4 slice. The times are simulated.
32 devices in a mesh: dp: 16 (over z, x, core), tensor: 2 (over y).
Axes of the slice: x: 2, y: 2, z: 4, core: 2. Of those that a mesh axis runs over, the one named last changes fastest.
Arguments:
- q_new: bfloat16 [2048, 8192], P(('dp', 'tensor')), may hold values from -6 to 6
- k_new: bfloat16 [2048, 1024], P(('dp', 'tensor')), may hold values from -8 to 8
- v_new: bfloat16 [2048, 1024], P(('dp', 'tensor')), may hold values from -6 to 6
- hist_kv: bfloat16 [512, 128, 2, 1024], P('dp', None, None, 'tensor'), may hold values from -8 to 8
- sources: int32 [16, 64, 1], P('dp'), may hold values from 0 to 15; in each aligned block of 64 rows (0 to 63, 64 to 127, ..., all dimensions but the last counted through in order) at most 8 rows name the same one
- block_ids: int32 [16, 64], P('dp'), may hold values from 0 to 31
- hist_len: int32 [16], P('dp'), may hold values from 1 to 64, 960 in all
Outputs:
- attended: bfloat16 [2048, 8192], P(('dp', 'tensor'))
Inputs may be any that keep to these rules, and one draw needn't show every extreme that they name: `sources`: in each group's list no owner is named in more than 8 slots, and some owner is named in exactly 8 slots. `hist_len`: some group has all 64 slots live.
All inputs are finite; a program needn't handle non-finite values.
Results may differ from a plain program's by a relative error of at most 0.0032.
Values may be sent and summed in bfloat16 or wider, within the bound.
A program may use at most 128 MiB of HBM per device.

v0:
```python
import math

import jax
import jax.numpy as jnp
from jax import lax
from jax.sharding import PartitionSpec as P

HQ = 64
KVH = 8
HD = 128


def slot_ranks(src_rows):
    count = src_rows.shape[-1]
    order = jnp.arange(count)
    earlier = order[None, :] < order[:, None]
    same = (src_rows[..., :, None] == src_rows[..., None, :]) & earlier
    return jnp.sum(same.astype(jnp.int32), axis=-1)


def owner_table(src_rows, id_rows, ranks, owners, capacity):
    match_owner = src_rows[..., None, :] == owners[:, None]
    slot_index = jnp.arange(capacity)
    match_rank = ranks[..., None, :] == slot_index[:, None]
    hitting = match_owner[..., :, None, :] & match_rank[..., None, :, :]
    return jnp.sum(jnp.where(hitting, id_rows[..., None, None, :], 0), axis=-1)


def local(q_new, k_new, v_new, hist_kv, sources, block_ids, hist_len):
    parts = lax.axis_size("tensor")
    groups = lax.axis_size("dp")
    tok_local, q_width = q_new.shape
    kv_width = k_new.shape[1]
    q_parts = q_new.reshape(tok_local, parts, q_width // parts)
    k_parts = k_new.reshape(tok_local, parts, kv_width // parts)
    v_parts = v_new.reshape(tok_local, parts, kv_width // parts)
    q_here, key_local_part, v_here = (
        lax.all_to_all(q_parts, "tensor", split_axis=1, concat_axis=0, tiled=True),
        lax.all_to_all(k_parts, "tensor", split_axis=1, concat_axis=0, tiled=True),
        lax.all_to_all(v_parts, "tensor", split_axis=1, concat_axis=0, tiled=True),
    )
    new_count = q_here.shape[0]
    kv_heads = kv_width // parts // HD
    per_kv = HQ // KVH
    query_rows = q_here.reshape(new_count, kv_heads, per_kv, HD)
    fresh_turn_keys = key_local_part.reshape(new_count, kv_heads, HD)
    fresh_turn_values = v_here.reshape(new_count, kv_heads, HD)
    src_list = sources.reshape(-1)
    slots = src_list.shape[0]
    capacity = max(2, 2 * slots // groups)
    ranks = slot_ranks(src_list)
    all_src, all_ids = (
        lax.all_gather(sources, "dp", axis=0, tiled=True),
        lax.all_gather(block_ids, "dp", axis=0, tiled=True),
    )
    all_src = all_src.reshape(groups, slots)
    owners = jnp.reshape(lax.axis_index("dp"), (1,))
    send_table = owner_table(all_src, all_ids, slot_ranks(all_src), owners, capacity).reshape(
        groups, capacity
    )
    picked = hist_kv[send_table.reshape(-1)]
    block_len = picked.shape[1]
    width = picked.shape[3]
    picked = picked.reshape(groups, capacity, block_len, 2, width)
    where_from = src_list * capacity + ranks
    arrived = lax.all_to_all(picked, "dp", split_axis=0, concat_axis=0, tiled=True)
    arrived = arrived.reshape(groups * capacity, block_len, 2, width)[where_from]
    hist_keys = arrived[:, :, 0]
    hist_vals = arrived[:, :, 1]
    score_scale = 1.0 / math.sqrt(HD)
    step = math.gcd(slots, 8)
    turns = slots // step
    key_blocks = hist_keys.reshape(turns, step * block_len, kv_heads, HD)
    val_blocks = hist_vals.reshape(turns, step * block_len, kv_heads, HD)
    live = jnp.repeat((jnp.arange(slots) < hist_len[0]).reshape(turns, step), block_len, axis=1)
    causal = jnp.arange(new_count)[:, None] >= jnp.arange(new_count)[None, :]
    fresh_turn_scores = (
        jnp.einsum(
            "fusi,pui->usfp", query_rows, fresh_turn_keys, preferred_element_type=jnp.float32
        )
        * score_scale
    )
    fresh_turn_scores = jnp.where(causal[None, None], fresh_turn_scores, -jnp.inf)

    def score_block(keys, mask):
        scores = (
            jnp.einsum("nhgd,khd->hgnk", query_rows, keys, preferred_element_type=jnp.float32)
            * score_scale
        )
        return jnp.where(mask[None, None, None, :], scores, -jnp.inf)

    def max_step(top, inputs):
        keys, mask = inputs
        return (jnp.maximum(top, jnp.max(score_block(keys, mask), axis=-1)), None)

    top, _ = lax.scan(max_step, jnp.max(fresh_turn_scores, axis=-1), (key_blocks, live))

    def sum_step(carry, inputs):
        total, running_sum = carry
        keys, vals, mask = inputs
        weights = jnp.exp(score_block(keys, mask) - top[..., None])
        total = total + jnp.sum(weights, axis=-1)
        running_sum = running_sum + jnp.einsum(
            "hgnk,khd->nhgd", weights.astype(jnp.bfloat16), vals, preferred_element_type=jnp.float32
        )
        return ((total, running_sum), None)

    new_weights = jnp.exp(fresh_turn_scores - top[..., None])
    start_total = jnp.sum(new_weights, axis=-1)
    start_summed = jnp.einsum(
        "vxyl,lvq->yvxq",
        new_weights.astype(jnp.bfloat16),
        fresh_turn_values,
        preferred_element_type=jnp.float32,
    )
    (total, running_sum), _ = lax.scan(
        sum_step, (start_total, start_summed), (key_blocks, val_blocks, live)
    )
    result = running_sum / jnp.transpose(total, (2, 0, 1))[..., None]
    result = result.astype(jnp.bfloat16).reshape(new_count, 1, kv_heads * per_kv * HD)
    back = lax.all_to_all(result, "tensor", split_axis=0, concat_axis=1, tiled=True)
    return back.reshape(tok_local, q_width)


def solution(mesh):
    return jax.shard_map(
        local,
        mesh=mesh,
        in_specs=(
            P(("dp", "tensor"), None),
            P(("dp", "tensor"), None),
            P(("dp", "tensor"), None),
            P("dp", None, None, "tensor"),
            P("dp", None, None),
            P("dp", None),
            P("dp"),
        ),
        out_specs=P(("dp", "tensor"), None),
        check_vma=False,
    )
```

profile of v0, /device:TPU:10, one launch (start us, length us, event | category | flops | bytes accessed | tf_op | source)
XLA Modules:
  0.0 1172.0 jit_solution(9809503238803412234)
XLA Ops:
  1.6 3.4 all-to-all-start
  4.9 15.2 %all_gather.6 = s32[16,64,1]{1,2,0:T(1,128)S(1)} all-gather(s32[1,64,1]{1,2,0:T(1,128)} %param.15), channel_id=1, replica_groups=mesh['dp'=16,'tensor'=2] {'dp'}, dimensions={0}, use_global_device_ids=true | all-gather | bytes 4352 | tf_op jit(solution)/shard_map/all_gather | solution.py:53
  20.1 2.3 copy.138
  24.0 21.3 %all-gather = s32[16,1,64]{2,1,0:T(1,128)S(1)} all-gather(s32[1,1,64]{2,1,0:T(1,128)} %bitcast.151), channel_id=1, replica_groups=mesh['dp'=16,'tensor'=2] {'dp'}, dimensions={0}, use_global_device_ids=true | all-gather | bytes 4352 | tf_op jit(solution)/shard_map/all_gather | solution.py:54
  45.3 3.4 all-to-all-start.3
  48.7 4.7 all-to-all-done.3
  53.4 3.6 all-to-all-start.1
  58.0 72.1 %gather_fusion = bf16[128,128,2,512]{3,2,1,0:T(2,128)(2,1)} fusion(bf16[32,128,2,512]{3,2,1,0:T(2,128)(2,1)} %param.14, s32[1024]{0:T(1024)S(1)} %pad_clamp_fusion.1), kind=kCustom, calls=%fused_computation | custom fusion | bytes 67109376 | tf_op jit(solution)/shard_map/gather | solution.py:61
  130.1 22.9 %copy.88 = bf16[16,8,128,2,512]{4,2,3,1,0:T(8,128)(2,1)} copy(bf16[16,8,128,2,512]{4,3,2,1,0:T(2,128)(2,1)} %bitcast.133) | data formatting | bytes 67108864 | tf_op jit(solution)/shard_map/reshape | solution.py:64
  153.0 8.1 all-to-all-start.2
  163.5 719.1 %all-to-all-done.2 = bf16[16,8,128,2,512]{4,2,3,1,0:T(8,128)(2,1)} async-done(((bf16[16,8,128,2,512]{4,2,3,1,0:T(8,128)(2,1)}), bf16[16,8,128,2,512]{4,2,3,1,0:T(8,128)(2,1)}, u32[]{:S(2)}, u32[]{:S(2)}) %all-to-all-start.2) | async-done | bytes 33554464 | tf_op jit(solution)/shard_map/all_to_all | solution.py:66
  882.6 11.8 %gather_fusion.1 = bf16[64,128,2,512]{3,1,2,0:T(8,128)(2,1)} fusion(bf16[128,128,2,512]{3,1,2,0:T(8,128)(2,1)} %bitcast.25, s32[1024]{0:T(1024)S(1)} %pad_clamp_fusion), kind=kCustom, calls=%fused_computation.1 | custom fusion | bytes 33554688 | tf_op jit(solution)/shard_map/gather | solution.py:67
  894.4 11.6 fusion.28
  906.0 12.5 %reshape.197 = bf16[8,1024,4,128]{3,2,1,0:T(4,128)(2,1)} reshape(bf16[64,128,1,512]{3,1,2,0:T(8,128)(2,1)} %get-tuple-element.180) | data formatting | bytes 16777216 | tf_op jit(solution)/shard_map/reshape;squeeze | solution.py:73
  918.6 8.7 copy.90
  927.2 29.3 %while.22 = (s32[]{:T(128)}, f32[4,8,128]{2,1,0:T(8,128)S(1)}, pred[8,1024]{1,0:T(8,128)(4,1)S(1)}, bf16[8,1024,4,128]{3,1,2,0:T(8,128)(2,1)}, bf16[128,4,8,128]{3,0,2,1:T(8,128)(2,1)S(1)}, /*index=5*/s32[]{:T(128)}) while((s32[]{:T(128)}, f32[4,8,128]{2,1,0:T(8,128)S(1)}, pred[8,1024]{1,0:T(8,128)(4,1)S(1)}, ...), condition=%wide.region_6.7_spmd, body=%wide.region_4.6_spmd.sunk | while | flops 1086324736 | bytes 2166345 | solution.py:96
  927.3 3.6 select_reduce_fusion.3
  930.9 3.6 select_reduce_fusion.3
  934.6 3.6 select_reduce_fusion.3
  938.2 3.6 select_reduce_fusion.3
  941.9 3.6 select_reduce_fusion.3
  945.6 3.6 select_reduce_fusion.3
  949.2 3.6 select_reduce_fusion.3
  952.9 3.6 select_reduce_fusion.3
  956.9 1.9 convolution_bitcast_fusion
  958.7 2.9 copy.96
  961.7 12.5 %reshape.198 = bf16[8,1024,4,128]{3,2,1,0:T(4,128)(2,1)} reshape(bf16[64,128,1,512]{3,1,2,0:T(8,128)(2,1)} %get-tuple-element.179) | data formatting | bytes 16777216 | tf_op jit(solution)/shard_map/reshape;squeeze | solution.py:74
  974.2 170.8 %while.23 = (s32[]{:T(128)}, f32[4,8,128]{2,1,0:T(8,128)S(1)}, f32[128,4,8,128]{0,3,2,1:T(8,128)}, pred[8,1024]{1,0:T(8,128)(4,1)S(1)}, bf16[8,1024,4,128]{3,1,2...) while((s32[]{:T(128)}, f32[4,8,128]{2,1,0:T(8,128)S(1)}, ...), condition=%wide.region_10.11_spmd, body=%wide.region_8.10_spmd.sunk | while | flops 2181562368 | bytes 45191780 | solution.py:116
  974.2 8.9 fusion.43
  983.2 1.6 constant_dynamic-slice_fusion.2
  985.4 10.1 bitcast_add_fusion.3
  995.6 8.9 fusion.43
  1006.8 10.1 bitcast_add_fusion.3
  1016.9 8.9 fusion.43
  1028.1 10.1 bitcast_add_fusion.3
  1038.3 8.9 fusion.43
  1047.2 1.6 constant_dynamic-slice_fusion.2
  1049.5 10.1 bitcast_add_fusion.3
  1059.6 8.9 fusion.43
  1070.8 10.1 bitcast_add_fusion.3
  1081.0 8.9 fusion.43
  1092.2 10.1 bitcast_add_fusion.3
  1102.3 8.9 fusion.43
  1113.5 10.1 bitcast_add_fusion.3
  1123.7 8.9 fusion.43
  1134.9 10.1 bitcast_add_fusion.3
  1145.0 1.8 divide_convert_fusion
  1150.2 17.1 %all_to_all.65 = bf16[2,2,131072]{2,1,0:T(2,128)(2,1)S(1)} all-to-all(bf16[2,2,131072]{2,1,0:T(2,128)(2,1)S(1)} %reshape.201), channel_id=1, replica_groups=mesh['dp'=16,'tensor'=2] {'tensor'}, dimensions={0} | all-to-all | bytes 2097152 | tf_op jit(solution)/shard_map/all_to_all | solution.py:121
  (79 shorter events, 29.5 us)
Async XLA Ops:
  1.6 43.8 %all-to-all-start = ((bf16[64,2,512]{2,0,1:T(8,128)(2,1)}), bf16[64,2,512]{2,0,1:T(8,128)(2,1)S(1)}, u32[]{:S(2)}, u32[]{:S(2)}) async-start(bf16[64,2,512]{2,0,1:T(8,128)(2,1)} %bitcast.113), calls=%async_computation | async-start | bytes 262144 | tf_op jit(solution)/shard_map/all_to_all | solution.py:39
  45.3 8.1 all-to-all-start.3
  53.4 99.6 %all-to-all-start.1 = ((bf16[64,2,4096]{2,0,1:T(8,128)(2,1)}), bf16[64,2,4096]{2,0,1:T(8,128)(2,1)S(1)}, u32[]{:S(2)}, u32[]{:S(2)}) async-start(bf16[64,2,4096]{2,0,1:T(8,128)(2,1)} %bitcast.111), calls=%async_computation.1 | async-start | bytes 2097152 | tf_op jit(solution)/shard_map/all_to_all | solution.py:38
  153.0 8.8 copy-start
  153.0 729.6 %all-to-all-start.2 = ((bf16[16,8,128,2,512]{4,2,3,1,0:T(8,128)(2,1)}), bf16[16,8,128,2,512]{4,2,3,1,0:T(8,128)(2,1)}, u32[]{:S(2)}, u32[]{:S(2)}) async-start(bf16[16,8,128,2,512]{4,2,3,1,0:T(8,128)(2,1)} %copy.88), calls=%async_computation.2 | async-start | bytes 67108864 | tf_op jit(solution)/shard_map/all_to_all | solution.py:66
where the time goes:
time: 1170 us
  waiting for transfers between devices  724 us (62%)
  local copies, waits for them, and re-layouts  186 us (16%)
  matrix products  184 us (16%)
  blocking collectives  53.7 us (5%)
  starting transfers between devices  18.4 us (2%)
    all_to_all x1, waiting for transfers between devices, local(): lax.all_to_all(picked, 'dp', split_axis=0, concat_axis=0, tiled=True)  719 us
    dot_general x16, matrix products, score_block(): jnp.einsum('nhgd,khd->hgnk', query_rows, keys, preferred_element_type=jnp...  100 us
    dot_general x8, matrix products, sum_step(): jnp.einsum('hgnk,khd->nhgd', weights.astype(jnp.bfloat16), vals, preferre...  81.1 us
    gather x1, local copies, waits for them, and re-layouts, local(): picked = hist_kv[send_table.reshape(-1)]  72.1 us
  transfers between devices with their start and end apart: 4, of which 2 were waited for; matrix products, arithmetic and copies ran while one was open for 9% of the time, Pallas kernels for 0%

commit v1 on v0

v1 whole, which is shorter than its diff:
```python
import functools
import math

import jax
import jax.numpy as jnp
from jax import lax
from jax.experimental import pallas as pl
from jax.experimental.pallas import tpu as pltpu
from jax.sharding import PartitionSpec as P

HD = 128
PER_KV = 8
ROWS = 1024
LOW = -1e30
SCALE = 1.4426950408889634 / math.sqrt(HD)
STEP = 256


def attend_kernel(width, counts, ids, own, q_ref, k_ref, vt_ref, o_ref, st_ref, s_scr, o_acc):
    g = pl.program_id(0)
    n = counts[g]
    total = n + own[g]
    heads = q_ref.shape[1]
    pieces = ROWS // STEP
    st_ref[...] = jnp.zeros_like(st_ref)
    for c in range(heads):

        def score(i, tops, causal):
            keys = k_ref[ids[g * width + i], c]
            out = []
            for j in range(pieces):
                cols = pl.ds(j * STEP, STEP)
                s = jnp.dot(keys, q_ref[0, c, :, cols], preferred_element_type=jnp.float32)
                if causal:
                    row = lax.broadcasted_iota(jnp.int32, s.shape, 0)
                    col = lax.broadcasted_iota(jnp.int32, s.shape, 1)
                    s = jnp.where(row <= col % 128, s, LOW)
                s_scr[i, :, cols] = s
                out.append(jnp.maximum(tops[j], jnp.max(s.reshape(16, 8, STEP), axis=0)))
            return tuple(out)

        tops = tuple(jnp.full((8, STEP), LOW, jnp.float32) for _ in range(pieces))
        tops = lax.fori_loop(0, n, functools.partial(score, causal=False), tops)
        tops = lax.fori_loop(n, total, functools.partial(score, causal=True), tops)

        @pl.when(total % 2 == 1)
        def _():
            s_scr[total] = jnp.zeros_like(s_scr[total])

        shift = [jnp.max(t, axis=0, keepdims=True) * SCALE for t in tops]
        o_acc[...] = jnp.zeros_like(o_acc)

        def gather(pair, sums):
            first = 2 * pair
            second = first + 1
            vt = jnp.concatenate(
                [vt_ref[ids[g * width + first], c], vt_ref[ids[g * width + second], c]], axis=1
            )
            out = []
            for j in range(pieces):
                cols = pl.ds(j * STEP, STEP)
                far = jnp.where(second < total, shift[j], -LOW)
                w0 = jnp.exp2(s_scr[first, :, cols] * SCALE - shift[j])
                w1 = jnp.exp2(s_scr[second, :, cols] * SCALE - far)
                w = jnp.concatenate([w0, w1], axis=0)
                out.append(sums[j] + jnp.sum(w.reshape(32, 8, STEP), axis=0))
                o_acc[:, cols] += jnp.dot(
                    vt, w.astype(jnp.bfloat16), preferred_element_type=jnp.float32
                )
            return tuple(out)

        sums = tuple(jnp.zeros((8, STEP), jnp.float32) for _ in range(pieces))
        sums = lax.fori_loop(0, (total + 1) // 2, gather, sums)
        o_ref[0, c] = o_acc[...].astype(jnp.bfloat16)
        for j in range(pieces):
            cols = pl.ds(j * STEP, STEP)
            st_ref[0, 2 * c : 2 * c + 1, cols] = shift[j]
            st_ref[0, 2 * c + 1 : 2 * c + 2, cols] = jnp.sum(sums[j], axis=0, keepdims=True)


def attend(counts, ids, own, q, keys, vals_t):
    groups, heads = q.shape[:2]
    width = ids.shape[1]
    return pl.pallas_call(
        functools.partial(attend_kernel, width),
        grid_spec=pltpu.PrefetchScalarGridSpec(
            num_scalar_prefetch=3,
            grid=(groups,),
            in_specs=[
                pl.BlockSpec((1, heads, HD, ROWS), lambda g, *_: (g, 0, 0, 0)),
                pl.BlockSpec(memory_space=pltpu.VMEM),
                pl.BlockSpec(memory_space=pltpu.VMEM),
            ],
            out_specs=[
                pl.BlockSpec((1, heads, HD, ROWS), lambda g, *_: (g, 0, 0, 0)),
                pl.BlockSpec((1, 8, ROWS), lambda g, *_: (g, 0, 0)),
            ],
            scratch_shapes=[
                pltpu.VMEM((width, 128, ROWS), jnp.float32),
                pltpu.VMEM((HD, ROWS), jnp.float32),
            ],
        ),
        out_shape=[
            jax.ShapeDtypeStruct(q.shape, jnp.bfloat16),
            jax.ShapeDtypeStruct((groups, 8, ROWS), jnp.float32),
        ],
        compiler_params=pltpu.CompilerParams(vmem_limit_bytes=48 * 1024 * 1024),
    )(counts, ids.reshape(-1), own, q, keys, vals_t)


def exchange(x, axis, groups=None, split=0, concat=0):
    return lax.all_to_all(
        x, axis, split_axis=split, concat_axis=concat, tiled=True, axis_index_groups=groups
    )


def local(q_new, k_new, v_new, hist_kv, sources, block_ids, hist_len):
    groups = lax.axis_size("dp")
    parts = lax.axis_size("tensor")
    tok = q_new.shape[0]
    new = parts * tok
    pool, block = hist_kv.shape[:2]
    slots = block_ids.shape[1]
    kv_heads = hist_kv.shape[3] // HD
    span = 2 if kv_heads % 2 == 0 else 1
    heads = kv_heads // span
    kv_cols = heads * HD
    q_cols = kv_cols * PER_KV
    units = groups // span
    mates = [list(range(span * i, span * i + span)) for i in range(units)]
    peers = [list(range(i, groups, span)) for i in range(span)]
    unit = lax.axis_index("dp") // span

    live = jnp.arange(slots)[None, :] < hist_len[:, None]
    code = jnp.where(live, sources.reshape(1, slots) * pool + block_ids, -1)
    code = lax.all_gather(code, "dp", axis=0, tiled=True)
    mine = (code >= 0) & (code // (span * pool) == unit)
    counts = jnp.sum(mine.astype(jnp.int32), axis=1)
    rank = jnp.cumsum(mine.astype(jnp.int32), axis=1) - 1
    width = min(span * max(2, 2 * slots // groups), slots) + 2
    hit = mine[:, None, :] & (rank[:, None, :] == jnp.arange(width)[None, :, None])
    ids = jnp.sum(jnp.where(hit, (code % (span * pool))[:, None, :], 0), axis=-1)
    order = jnp.arange(groups)
    own = (order // span == unit).astype(jnp.int32)
    extra = (jnp.arange(width)[None, :] == counts[:, None]) & (own[:, None] == 1)
    ids = jnp.where(extra, span * pool + (order % span)[:, None], ids)

    share = parts * span
    turn = jnp.concatenate([x.reshape(tok, share, -1) for x in (q_new, k_new, v_new)], axis=2)
    turn = exchange(turn.reshape(tok, parts, -1), "tensor", split=1)
    turn = turn.reshape(new, span, -1).transpose(1, 0, 2)
    if span > 1:
        turn = exchange(turn, "dp", mates)
    q_t = turn[:, :, :q_cols].reshape(span, new, heads, PER_KV, HD).transpose(0, 2, 4, 3, 1)
    q_t = q_t.reshape(span, heads, HD, PER_KV * new)
    fresh = turn[:, :, q_cols:].reshape(span, new, 2, heads, HD)
    k_fresh = fresh[:, :, 0].transpose(0, 2, 1, 3)
    v_fresh = fresh[:, :, 1].transpose(0, 2, 3, 1)
    q_all = lax.all_gather(q_t, "dp", axis=0, tiled=True, axis_index_groups=peers)

    halves = hist_kv.reshape(pool, block, 2, span, kv_cols).transpose(3, 0, 2, 1, 4)
    if span > 1:
        halves = exchange(halves, "dp", mates)
    halves = halves.reshape(span * pool, 2, block, heads, HD)
    keys = jnp.concatenate([halves[:, 0].transpose(0, 2, 1, 3), k_fresh], axis=0)
    vals_t = jnp.concatenate([halves[:, 1].transpose(0, 2, 3, 1), v_fresh], axis=0)

    part, stats = attend(counts, ids, own, q_all, keys, vals_t)

    part = part.reshape(units, span, heads, HD, ROWS)
    stats = stats[:, : 2 * heads].reshape(units, span, heads, 2, ROWS)
    part = exchange(part, "dp", peers)
    stats = exchange(stats, "dp", peers)
    shift, sums = stats[:, :, :, 0], stats[:, :, :, 1]
    scale = jnp.exp2(shift - jnp.max(shift, axis=0, keepdims=True))
    scale = scale / jnp.sum(scale * sums, axis=0, keepdims=True)
    result = jnp.sum(part.astype(jnp.float32) * scale[:, :, :, None, :], axis=0)
    result = result.astype(jnp.bfloat16)
    result = result.reshape(span, heads, HD, PER_KV, new).transpose(0, 4, 1, 3, 2)
    result = result.reshape(span, new, q_cols)
    if span > 1:
        result = exchange(result, "dp", mates)
    result = result.transpose(1, 0, 2).reshape(new, 1, span * q_cols)
    result = exchange(result, "tensor", split=0, concat=1)
    return result.reshape(tok, share * q_cols)


def solution(mesh):
    return jax.shard_map(
        local,
        mesh=mesh,
        in_specs=(
            P(("dp", "tensor"), None),
            P(("dp", "tensor"), None),
            P(("dp", "tensor"), None),
            P("dp", None, None, "tensor"),
            P("dp", None, None),
            P("dp", None),
            P("dp"),
        ),
        out_specs=P(("dp", "tensor"), None),
        check_vma=False,
    )
```

time: 1170 us -> 559 us (0.48)
  the two profiles are of different devices: /device:TPU:10 before, /device:TPU:0 now
where the time goes in v1:
time: 559 us; the launch traced here: 563 us
  waiting for transfers between devices  217 us (39%)
  Pallas kernels  152 us (27%)
  blocking collectives  80.4 us (14%)
  local copies, waits for them, and re-layouts  68.8 us (12%)
  other arithmetic  18.2 us (3%)
  between operations  14.3 us (3%)
  starting transfers between devices  12.3 us (2%)
    all_to_all x2, waiting for transfers between devices, exchange(): lax.all_to_all(x, axis, split_axis=split, concat_axis=concat, tiled=True,...  181 us
    pallas_call x1, Pallas kernels, attend(): pl.pallas_call(functools.partial(attend_kernel, width), grid_spec=pltpu.P...  152 us
    all_to_all x5, blocking collectives, exchange(): lax.all_to_all(x, axis, split_axis=split, concat_axis=concat, tiled=True,...  58.6 us
    all_gather x1, waiting for transfers between devices, local(): lax.all_gather(q_t, 'dp', axis=0, tiled=True, axis_index_groups=peers)  36.4 us
    unnamed x14, local copies, waits for them, and re-layouts  29.3 us
    all_gather x1, blocking collectives, local(): code = lax.all_gather(code, 'dp', axis=0, tiled=True)  21.7 us
    all_to_all x2, starting transfers between devices, exchange(): lax.all_to_all(x, axis, split_axis=split, concat_axis=concat, tiled=True,...  12.3 us
  transfers between devices with their start and end apart: 3, of which 2 were waited for; matrix products, arithmetic and copies ran while one was open for 11% of the time, Pallas kernels for 0%

profile of v1, /device:TPU:0, one launch (start us, length us, event | category | flops | bytes accessed | tf_op | source)
XLA Modules:
  0.0 563.2 jit_solution(9051816931617761550)
XLA Ops:
  6.5 1.8 reshape.125
  8.4 1.0 reshape.126
  9.4 1.0 reshape.127
  10.4 0.6 pad_maximum_fusion.2
  11.0 0.9 reshape.128
  11.9 0.2 copy.83
  12.1 20.4 %all_to_all.55 = bf16[64,2,5120]{2,0,1:T(8,128)(2,1)S(1)} all-to-all(bf16[64,2,5120]{2,0,1:T(8,128)(2,1)S(1)} %copy.83), channel_id=1, replica_groups=mesh['dp'=16,'tensor'=2] {'tensor'}, dimensions={1} | all-to-all | bytes 2621440 | tf_op jit(solution)/shard_map/all_to_all | solution.py:112
  32.6 1.0 reshape.129
  33.6 0.1 copy.84
  33.7 4.8 all_to_all.56
  38.6 0.7 copy.102
  39.3 0.7 copy.86
  40.0 1.3 copy.87
  41.3 21.3 %copy.88 = bf16[32,128,2,512]{1,3,2,0:T(8,128)(2,1)} copy(bf16[32,128,2,512]{3,2,1,0:T(2,128)(2,1)} %param.10) | data formatting | bytes 16777216 | tf_op args[3]
  62.6 7.7 %copy.89 = bf16[2,32,2,128,256]{3,4,1,2,0:T(8,128)(2,1)} copy(bf16[2,32,2,128,256]{3,4,0,2,1:T(8,128)(2,1)} %bitcast.76) | data formatting | bytes 16777216 | tf_op jit(solution)/shard_map/transpose | solution.py:161
  70.3 7.1 %all-to-all-start.2 = ((bf16[2,32,2,128,256]{3,4,1,2,0:T(8,128)(2,1)}), bf16[2,32,2,128,256]{3,4,1,2,0:T(8,128)(2,1)}, u32[]{:S(2)}, u32[]{:S(2)}) async-start(bf16[2,32,2,128,256]{3,4,1,2,0:T(8,128)(2,1)} %copy.89), calls=%async_computation.2 | async-start | bytes 16777216 | tf_op jit(solution)/shard_map/all_to_all | solution.py:112
  78.2 21.7 %all-gather = s32[16,1,64]{2,1,0:T(1,128)S(1)} all-gather(s32[1,1,64]{2,1,0:T(1,128)S(1)} %fusion.10), channel_id=1, replica_groups=mesh['dp'=16,'tensor'=2] {'dp'}, dimensions={0}, use_global_device_ids=true | all-gather | bytes 4352 | tf_op jit(solution)/shard_map/all_gather | solution.py:136
  99.9 0.2 reduce_window_sum.11
  100.2 0.4 select_reduce_fusion
  100.8 7.7 %copy.90 = bf16[2,32,2,128,256]{3,4,1,0,2:T(8,128)(2,1)} copy(bf16[2,32,2,128,256]{3,4,1,2,0:T(8,128)(2,1)} %all-to-all-done.2) | data formatting | bytes 16777216 | tf_op jit(solution)/shard_map/all_to_all | solution.py:112
  108.6 6.1 %slice_bitcast_fusion = (bf16[64,2,128,128]{3,2,1,0:T(8,128)(2,1)}, bf16[64,2,128,128]{2,3,1,0:T(8,128)(2,1)}) fusion(bf16[64,2,128,2,128]{2,4,3,0,1:T(8,128)(2,1)} %bitcast.75), kind=kLoop, calls=%fused_computation.3 | loop fusion | bytes 16777216 | tf_op jit(solution)/shard_map/transpose | solution.py:166
  114.7 0.2 copy.103
  114.9 4.6 pad_maximum_fusion
  119.5 6.4 %copy.94.k_ref = bf16[66,2,128,128]{3,2,1,0:T(8,128)(2,1)} copy(bf16[66,2,128,128]{2,3,1,0:T(8,128)(2,1)} %pad_maximum_fusion) | data formatting | bytes 8650752 | tf_op jit(solution)/shard_map/concatenate | solution.py:165
  125.9 4.5 pad_maximum_fusion.1.vt_ref
  130.4 36.4 %all-gather.3.cloned.1.call-done.q_ref = bf16[16,2,128,1024]{3,2,1,0:T(8,128)(2,1)} async-done(((bf16[2,2,128,1024]{3,2,1,0:T(8,128)(2,1)}), bf16[16,2,128,1024]{3,2,1,0:T(8,128)(2,1)}) %all-gather.3.cloned.1.call-update) | async-done | bytes 8388624 | tf_op jit(solution)/shard_map/all_gather | solution.py:159
  166.8 2.2 copy-done
  169.0 151.9 %shard_map.73 = (bf16[16,2,128,1024]{3,2,1,0:T(8,128)(2,1)}, f32[16,8,1024]{2,1,0:T(8,128)S(1)}) custom-call(s32[16]{0:T(128)S(1)} %convert_reduce_fusion.counts, s32[288]{0:T(512)S(1)} %select_n.59.ids, s32[16]{0:T(128)S(1)} %compare_convert_fusion.own, bf16[16,2,128,1024]{3,2,1,0:T(8,128)(2,1)} %all-gather.3.cloned.1.call-done.q_ref, ...), custom_call_target="tpu_custom_call" | custom-call | tf_op jit(solution)/shard_map/pallas_call | solution.py:84
  320.9 0.2 reshape.136
  321.2 12.2 %all_to_all.57 = f32[8,2,2,2,1024]{4,3,2,1,0:T(2,128)S(1)} all-to-all(f32[8,2,2,2,1024]{4,3,2,1,0:T(2,128)S(1)} %reshape.136), channel_id=1, replica_groups={{0,4,8,12,16,20,24,28},{2,6,10,14,18,22,26,30},{1,5,9,13,17,21,25,29},{..., dimensions={0} | all-to-all | bytes 524288 | tf_op jit(solution)/shard_map/all_to_all | solution.py:112
  333.4 5.1 all-to-all-start.3
  338.5 0.3 slice_reduce_fusion
  338.8 0.2 fusion.1
  339.0 0.1 divide_bitcast_fusion
  339.1 181.0 %all-to-all-done.3 = bf16[8,2,2,128,1024]{4,3,2,1,0:T(8,128)(2,1)} async-done(((bf16[8,2,2,128,1024]{4,3,2,1,0:T(8,128)(2,1)}), bf16[8,2,2,128,1024]{4,3,2,1,0:T(8,128)(2,1)}, u32[]{:S(2)}, u32[]{:S(2)}) %all-to-all-start.3) | async-done | bytes 8388640 | tf_op jit(solution)/shard_map/all_to_all | solution.py:112
  520.1 5.7 %multiply_reduce_fusion = bf16[2,2,128,1024]{3,2,1,0:T(8,128)(2,1)S(1)} fusion(bf16[8,2,2,128,1024]{4,3,2,1,0:T(8,128)(2,1)} %all-to-all-done.3, f32[8,2,2,1024]{3,2,1,0:T(2,128)S(1)} %divide_bitcast_fusion), kind=kLoop, calls=%fused_computation | loop fusion | flops 12058624 | bytes 9568256 | tf_op jit(solution)/shard_map/reduce_sum | solution.py:177
  525.8 0.7 copy.96
  526.5 0.7 copy.97
  527.1 4.6 all_to_all.58
  531.7 0.5 broadcast.134
  532.2 1.4 reduce.1
  533.7 0.5 copy.112
  534.2 0.8 reshape.142
  535.0 16.6 %all_to_all.59 = bf16[2,2,131072]{2,1,0:T(2,128)(2,1)S(1)} all-to-all(bf16[2,2,131072]{2,1,0:T(2,128)(2,1)S(1)} %reshape.142), channel_id=1, replica_groups=mesh['dp'=16,'tensor'=2] {'tensor'}, dimensions={0} | all-to-all | bytes 2097152 | tf_op jit(solution)/shard_map/all_to_all | solution.py:112
  551.6 0.9 reshape.143
  552.6 1.1 copy.101
  553.7 1.1 copy.99
  554.8 1.6 copy.108
  (22 shorter events, 0.6 us)
Async XLA Ops:
  6.5 160.3 %all-gather.3.cloned.1.call-start = ((), (), s32[]{:S(2)}) async-start(), calls=%async_computation.7 | async-start | bytes 9437184 | tf_op jit(solution)/shard_map/all_gather | solution.py:159
  70.3 7.8 %copy-start.1 = (s32[1,64]{1,0:T(1,128)S(1)}, s32[1,64]{1,0:T(1,128)}, u32[]{:S(2)}) copy-start(s32[1,64]{1,0:T(1,128)} %param.12) | copy-start | bytes 772
  70.3 7.8 %copy-start.2 = (s32[1,64,1]{1,2,0:T(1,128)S(1)}, s32[1,64,1]{1,2,0:T(1,128)}, u32[]{:S(2)}) copy-start(s32[1,64,1]{1,2,0:T(1,128)} %param.11) | copy-start | bytes 772
  70.3 30.5 %all-to-all-start.2 = ((bf16[2,32,2,128,256]{3,4,1,2,0:T(8,128)(2,1)}), bf16[2,32,2,128,256]{3,4,1,2,0:T(8,128)(2,1)}, u32[]{:S(2)}, u32[]{:S(2)}) async-start(bf16[2,32,2,128,256]{3,4,1,2,0:T(8,128)(2,1)} %copy.89), calls=%async_computation.2 | async-start | bytes 16777216 | tf_op jit(solution)/shard_map/all_to_all | solution.py:112
  166.8 2.2 copy-start
  333.4 186.7 %all-to-all-start.3 = ((bf16[8,2,2,128,1024]{4,3,2,1,0:T(8,128)(2,1)}), bf16[8,2,2,128,1024]{4,3,2,1,0:T(8,128)(2,1)}, u32[]{:S(2)}, u32[]{:S(2)}) async-start(bf16[8,2,2,128,1024]{4,3,2,1,0:T(8,128)(2,1)} %bitcast.77), calls=%async_computation.3 | async-start | bytes 16777216 | tf_op jit(solution)/shard_map/all_to_all | solution.py:112
Sparse Core Ops, SparseCore 0:
  41.4 125.3 all-gather.2

commit v2 on v1

v2 whole, which is shorter than its diff:
```python
import functools
import math

import jax
import jax.numpy as jnp
from jax import lax
from jax.experimental import pallas as pl
from jax.experimental.pallas import tpu as pltpu
from jax.sharding import PartitionSpec as P

HD = 128
PER_KV = 8
ROWS = 1024
LOW = -1e30
SCALE = 1.4426950408889634 / math.sqrt(HD)
STEP = 256
EXTRA = 16


def attend_kernel(width, fresh, qsel, gsel, counts, ids, q_ref, k_ref, vt_ref, *rest):
    if fresh:
        kf_ref, vf_ref, *rest = rest
    o_ref, q_t, acc = rest[-3:]
    i = pl.program_id(0)
    g = gsel[i]
    n = counts[g]
    heads = o_ref.shape[1]
    tiles = [(c, j) for c in range(heads) for j in range(ROWS // STEP)]

    for c in range(heads):
        for h in range(PER_KV):
            at = (c * PER_KV + h) * HD
            q_t[c, :, h * 128 : (h + 1) * 128] = q_ref[0, :, at : at + HD].T

    def fold(keys, vals_t, mask, second, carry):
        out = []
        for (c, j), (top, total) in zip(tiles, carry):
            cols = pl.ds(j * STEP, STEP)
            s = jnp.dot(keys[c], q_t[c, :, cols], preferred_element_type=jnp.float32)
            if mask is not None:
                s = jnp.where(mask, s, LOW)
            here = jnp.max(s[:128], axis=0, keepdims=True)
            if second is not None:
                there = jnp.max(s[128:], axis=0, keepdims=True)
                here = jnp.maximum(here, jnp.where(second, there, LOW))
            new = jnp.maximum(top, here * SCALE)
            w = jnp.exp2(s[:128] * SCALE - new)
            if second is not None:
                far = jnp.where(second, new, -LOW)
                w = jnp.concatenate([w, jnp.exp2(s[128:] * SCALE - far)], axis=0)
            fade = jnp.exp2(top - new)
            total = total * fade + jnp.sum(w.reshape(w.shape[0] // 8, 8, STEP), axis=0)
            acc[c, :, cols] = acc[c, :, cols] * fade + jnp.dot(
                vals_t[c], w.astype(jnp.bfloat16), preferred_element_type=jnp.float32
            )
            out.append((new, total))
        return tuple(out)

    acc[...] = jnp.zeros_like(acc)
    carry = tuple(
        (jnp.full((1, STEP), LOW, jnp.float32), jnp.zeros((8, STEP), jnp.float32)) for _ in tiles
    )
    if fresh:
        row = lax.broadcasted_iota(jnp.int32, (128, STEP), 0)
        col = lax.broadcasted_iota(jnp.int32, (128, STEP), 1)
        carry = fold(
            [kf_ref[i, c] for c in range(heads)],
            [vf_ref[i, c] for c in range(heads)],
            row <= col % 128,
            None,
            carry,
        )

    def pair(p, carry):
        one, two = ids[g * width + 2 * p], ids[g * width + 2 * p + 1]
        return fold(
            [jnp.concatenate([k_ref[one, c], k_ref[two, c]], axis=0) for c in range(heads)],
            [jnp.concatenate([vt_ref[one, c], vt_ref[two, c]], axis=1) for c in range(heads)],
            None,
            2 * p + 1 < n,
            carry,
        )

    carry = lax.fori_loop(0, (n + 1) // 2, pair, carry)
    for (c, j), (top, total) in zip(tiles, carry):
        cols = pl.ds(j * STEP, STEP)
        total = jnp.sum(total, axis=0, keepdims=True)
        some = total > 0.0
        safe = jnp.where(some, total, 1.0)
        o_ref[0, c, :HD, cols] = (acc[c, :, cols] / safe).astype(o_ref.dtype)
        left = jnp.where(some, top + jnp.log2(safe), LOW)
        row = lax.broadcasted_iota(jnp.int32, (EXTRA, STEP), 0)
        terms = jnp.zeros((EXTRA, STEP), jnp.float32)
        for k in range(3):
            term = left.astype(jnp.bfloat16).astype(jnp.float32)
            terms = jnp.where(row == k, term, terms)
            left = left - term
        o_ref[0, c, HD:, cols] = terms.astype(o_ref.dtype)


def attend(qsel, gsel, counts, ids, q, keys, vals_t, fresh=None, after=None):
    count = qsel.shape[0]
    heads = keys.shape[1]
    width = ids.shape[1]
    extra = () if fresh is None else fresh
    behind = () if after is None else (after,)
    work = count * 8 * heads * ROWS * 128
    return pl.pallas_call(
        functools.partial(attend_kernel, width, fresh is not None),
        grid_spec=pltpu.PrefetchScalarGridSpec(
            num_scalar_prefetch=4,
            grid=(count,),
            in_specs=[pl.BlockSpec((1,) + q.shape[1:], lambda i, qs, *_: (qs[i], 0, 0))]
            + [pl.BlockSpec(memory_space=pltpu.VMEM)] * (2 + len(extra))
            + [pl.BlockSpec(memory_space=pl.ANY)] * len(behind),
            out_specs=pl.BlockSpec((1, heads, HD + EXTRA, ROWS), lambda i, *_: (i, 0, 0, 0)),
            scratch_shapes=[
                pltpu.VMEM((heads, HD, ROWS), jnp.bfloat16),
                pltpu.VMEM((heads, HD, ROWS), jnp.float32),
            ],
        ),
        out_shape=jax.ShapeDtypeStruct(
            (count, heads, HD + EXTRA, ROWS), jnp.bfloat16 if fresh is None else jnp.float32
        ),
        compiler_params=pltpu.CompilerParams(vmem_limit_bytes=28 * 1024 * 1024),
        cost_estimate=pl.CostEstimate(
            flops=4 * HD * work, bytes_accessed=4 * count * heads * HD * ROWS, transcendentals=work
        ),
    )(qsel, gsel, counts, ids.reshape(-1), q, keys, vals_t, *extra, *behind)


def exchange(x, axis, groups=None, split=0, concat=0):
    return lax.all_to_all(
        x, axis, split_axis=split, concat_axis=concat, tiled=True, axis_index_groups=groups
    )


def local(q_new, k_new, v_new, hist_kv, sources, block_ids, hist_len):
    groups = lax.axis_size("dp")
    parts = lax.axis_size("tensor")
    tok = q_new.shape[0]
    new = parts * tok
    pool, block = hist_kv.shape[:2]
    slots = block_ids.shape[1]
    kv_heads = hist_kv.shape[3] // HD
    span = 2 if kv_heads % 2 == 0 else 1
    heads = kv_heads // span
    kv_cols = heads * HD
    q_cols = kv_cols * PER_KV
    units = groups // span
    mates = [list(range(span * i, span * i + span)) for i in range(units)]
    peers = [list(range(i, groups, span)) for i in range(span)]
    unit = lax.axis_index("dp") // span

    live = jnp.arange(slots)[None, :] < hist_len[:, None]
    code = jnp.where(live, sources.reshape(1, slots) * pool + block_ids, -1)
    code = lax.all_gather(code, "dp", axis=0, tiled=True)
    mine = (code >= 0) & (code // (span * pool) == unit)
    counts = jnp.sum(mine.astype(jnp.int32), axis=1)
    rank = jnp.cumsum(mine.astype(jnp.int32), axis=1) - 1
    width = min(span * max(2, 2 * slots // groups), slots) + 2
    hit = mine[:, None, :] & (rank[:, None, :] == jnp.arange(width)[None, :, None])
    ids = jnp.sum(jnp.where(hit, (code % (span * pool))[:, None, :], 0), axis=-1)

    share = parts * span
    turn = jnp.concatenate([x.reshape(tok, share, -1) for x in (q_new, k_new, v_new)], axis=2)
    turn = exchange(turn.reshape(tok, parts, -1), "tensor", split=1)
    turn = turn.reshape(new, span, -1).transpose(1, 0, 2)
    if span > 1:
        turn = exchange(turn, "dp", mates)
    q = turn[:, :, :q_cols]
    q_all = lax.all_gather(q, "dp", axis=0, tiled=True, axis_index_groups=peers)
    fresh = turn[:, :, q_cols:].reshape(span, new, 2, heads, HD)
    k_fresh = fresh[:, :, 0].transpose(0, 2, 1, 3)
    v_fresh = fresh[:, :, 1].transpose(0, 2, 3, 1)

    halves = hist_kv.reshape(pool, block, 2, span, kv_cols).transpose(3, 0, 2, 1, 4)
    if span > 1:
        halves = exchange(halves, "dp", mates)
    halves = halves.reshape(span * pool, 2, block, heads, HD)
    keys = halves[:, 0].transpose(0, 2, 1, 3)
    vals_t = halves[:, 1].transpose(0, 2, 3, 1)

    core = jnp.arange(span, dtype=jnp.int32)
    own = attend(core, unit * span + core, counts, ids, q, keys, vals_t, (k_fresh, v_fresh))
    arrived, sent = [own], []
    apart = list(range(units - 1, 0, -1))
    per = max(1, units // 8)
    for at in range(0, len(apart), per):
        some = apart[at : at + per]
        sel = jnp.concatenate([(unit ^ r) * span + core for r in some])
        after = own if len(sent) < 4 else sent[-4]
        part = attend(sel, sel, counts, ids, q_all, keys, vals_t, after=after)
        for k, r in enumerate(some):
            to = [(u * span + c, (u ^ r) * span + c) for u in range(units) for c in range(span)]
            arrived.append(lax.ppermute(part[k * span : (k + 1) * span], "dp", to))
        sent.append(arrived[-1])
    arrived = [x.astype(jnp.float32) for x in arrived]
    lses = [x[:, :, HD] + x[:, :, HD + 1] + x[:, :, HD + 2] for x in arrived]
    top = functools.reduce(jnp.maximum, lses)
    scales = [jnp.exp2(lse - top) for lse in lses]
    total = sum(scales)
    result = sum(x[:, :, :HD] * (w / total)[:, :, None, :] for x, w in zip(arrived, scales))
    result = result.astype(jnp.bfloat16)
    result = result.reshape(span, heads, HD, PER_KV, new).transpose(0, 4, 1, 3, 2)
    result = result.reshape(span, new, q_cols)
    if span > 1:
        result = exchange(result, "dp", mates)
    result = result.transpose(1, 0, 2).reshape(new, 1, span * q_cols)
    result = exchange(result, "tensor", split=0, concat=1)
    return result.reshape(tok, share * q_cols)


def solution(mesh):
    return jax.shard_map(
        local,
        mesh=mesh,
        in_specs=(
            P(("dp", "tensor"), None),
            P(("dp", "tensor"), None),
            P(("dp", "tensor"), None),
            P("dp", None, None, "tensor"),
            P("dp", None, None),
            P("dp", None),
            P("dp"),
        ),
        out_specs=P(("dp", "tensor"), None),
        check_vma=False,
    )
```

time: 559 us -> 487 us (0.87); the launches traced: 563 us -> 484 us
  waiting for transfers between devices: 217 us -> 79.4 us
  starting transfers between devices: 12.3 us -> 86 us
  local copies, waits for them, and re-layouts: 68.8 us -> 87.5 us
  Pallas kernels: 152 us -> 136 us
  blocking collectives: 80.4 us -> 68.1 us
    all_to_all x2 -> x1, waiting for transfers between devices: 181 us -> 0.01 us  [exchange(): lax.all_to_all(x, axis, split_axis=split, concat_axis=concat, tiled=True,...]
    ppermute x0 -> x7, starting transfers between devices: none -> 78.9 us  [local(): arrived.append(lax.ppermute(part[k * span:(k + 1) * span], 'dp', to))]
    ppermute x0 -> x7, waiting for transfers between devices: none -> 58.4 us  [local(): arrived.append(lax.ppermute(part[k * span:(k + 1) * span], 'dp', to))]
    unnamed x14 -> x51, local copies, waits for them, and re-layouts: 29.3 us -> 51.3 us
    pallas_call x1 -> x8, Pallas kernels: 152 us -> 136 us  [attend(): pl.pallas_call(functools.partial(attend_kernel, width, fresh is not None)...]
    all_gather x1, waiting for transfers between devices: 36.4 us -> 21 us  [local(): q_all = lax.all_gather(q, 'dp', axis=0, tiled=True, axis_index_groups=peers)]
    all_to_all x5 -> x4, blocking collectives: 58.6 us -> 46.4 us  [exchange(): lax.all_to_all(x, axis, split_axis=split, concat_axis=concat, tiled=True,...]
    concatenate x2 -> x0, other arithmetic: 9.14 us -> none  [the longest x1 4.6 us: local(): jnp.concatenate([halves[:, 0].transpose(0, 2, 1, 3), k_fresh], axis=0)]
  transfers between devices with their start and end apart: 3 -> 9, of which waited for: 2 -> 5; matrix products, arithmetic and copies ran while one was open for 11% -> 12% of each run, Pallas kernels for 0% -> 24%
where the time goes in v2:
time: 487 us; the launch traced here: 484 us
  Pallas kernels  136 us (28%)
  local copies, waits for them, and re-layouts  87.5 us (18%)
  starting transfers between devices  86 us (18%)
  waiting for transfers between devices  79.4 us (16%)
  blocking collectives  68.1 us (14%)
  between operations  14.5 us (3%)
  other arithmetic  13.2 us (3%)
    pallas_call x8, Pallas kernels, attend(): pl.pallas_call(functools.partial(attend_kernel, width, fresh is not None)...  136 us
    ppermute x7, starting transfers between devices, local(): arrived.append(lax.ppermute(part[k * span:(k + 1) * span], 'dp', to))  78.9 us
    ppermute x7, waiting for transfers between devices, local(): arrived.append(lax.ppermute(part[k * span:(k + 1) * span], 'dp', to))  58.4 us
    unnamed x51, local copies, waits for them, and re-layouts  51.3 us
    all_to_all x4, blocking collectives, exchange(): lax.all_to_all(x, axis, split_axis=split, concat_axis=concat, tiled=True,...  46.4 us
    all_gather x1, blocking collectives, local(): code = lax.all_gather(code, 'dp', axis=0, tiled=True)  21.7 us
    all_gather x1, waiting for transfers between devices, local(): q_all = lax.all_gather(q, 'dp', axis=0, tiled=True, axis_index_groups=peers)  21 us
  transfers between devices with their start and end apart: 9, of which 5 were waited for; matrix products, arithmetic and copies ran while one was open for 12% of the time, Pallas kernels for 24%

profile of v2, /device:TPU:0, one launch (start us, length us, event | category | flops | bytes accessed | tf_op | source)
XLA Modules:
  0.0 484.3 jit_solution(7791428261921451310)
XLA Ops:
  6.5 1.9 reshape.84
  10.4 20.4 %all_to_all.45 = bf16[64,2,5120]{2,0,1:T(8,128)(2,1)S(1)} all-to-all(bf16[64,2,5120]{2,0,1:T(8,128)(2,1)S(1)} %copy.106), channel_id=1, replica_groups=mesh['dp'=16,'tensor'=2] {'tensor'}, dimensions={1} | all-to-all | bytes 2621440 | tf_op jit(solution)/shard_map/all_to_all | solution.py:133
  31.9 4.8 all_to_all.46
  36.7 1.1 slice.152.q_ref
  37.9 21.3 %copy.108 = bf16[32,128,2,512]{1,3,2,0:T(8,128)(2,1)} copy(bf16[32,128,2,512]{3,2,1,0:T(2,128)(2,1)} %param.10) | data formatting | bytes 16777216 | tf_op args[3]
  59.1 7.8 %copy.109 = bf16[2,32,2,128,256]{3,4,1,2,0:T(8,128)(2,1)} copy(bf16[2,32,2,128,256]{3,4,0,2,1:T(8,128)(2,1)} %bitcast.87) | data formatting | bytes 16777216 | tf_op jit(solution)/shard_map/transpose | solution.py:177
  67.0 7.2 %all-to-all-start.2 = ((bf16[2,32,2,128,256]{3,4,1,2,0:T(8,128)(2,1)}), bf16[2,32,2,128,256]{3,4,1,2,0:T(8,128)(2,1)}, u32[]{:S(2)}, u32[]{:S(2)}) async-start(bf16[2,32,2,128,256]{3,4,1,2,0:T(8,128)(2,1)} %copy.109), calls=%async_computation.2 | async-start | bytes 16777216 | tf_op jit(solution)/shard_map/all_to_all | solution.py:133
  74.8 21.7 %all-gather = s32[16,1,64]{2,1,0:T(1,128)S(1)} all-gather(s32[1,1,64]{2,1,0:T(1,128)S(1)} %fusion.13), channel_id=1, replica_groups=mesh['dp'=16,'tensor'=2] {'dp'}, dimensions={0}, use_global_device_ids=true | all-gather | bytes 4352 | tf_op jit(solution)/shard_map/all_gather | solution.py:157
  97.3 7.8 %copy.110 = bf16[2,32,2,128,256]{3,4,1,0,2:T(8,128)(2,1)} copy(bf16[2,32,2,128,256]{3,4,1,2,0:T(8,128)(2,1)} %all-to-all-done.2) | data formatting | bytes 16777216 | tf_op jit(solution)/shard_map/all_to_all | solution.py:133
  105.1 6.2 %slice_bitcast_fusion = (bf16[64,2,128,128]{3,2,1,0:T(8,128)(2,1)}, bf16[64,2,128,128]{2,3,1,0:T(8,128)(2,1)}) fusion(bf16[64,2,128,2,128]{2,4,3,0,1:T(8,128)(2,1)} %bitcast.86), kind=kLoop, calls=%fused_computation | loop fusion | bytes 16777216 | tf_op jit(solution)/shard_map/transpose | solution.py:182
  111.3 6.4 %copy.114.k_ref = bf16[64,2,128,128]{3,2,1,0:T(8,128)(2,1)} copy(bf16[64,2,128,128]{2,3,1,0:T(8,128)(2,1)} %get-tuple-element.18) | data formatting | bytes 8388608 | tf_op jit(solution)/shard_map/transpose | solution.py:181
  119.5 2.2 copy-done.3
  121.7 2.2 copy-done.6
  125.4 17.0 %shard_map.73.rest_0_ = f32[2,2,144,1024]{3,2,1,0:T(8,128)S(1)} custom-call(s32[2]{0:T(128)S(1)} %iota.27.qsel, s32[2]{0:T(128)S(1)} %copy-done.11, s32[16]{0:T(128)S(1)} %convert_reduce_fusion.counts, s32[288]{0:T(512)S(1)} %reshape.83.ids, bf16[2,128,2048]{2,1,0:T(8,128)(2,1)S(1)} %copy-done.9, bf16[64,2,128,128]{3,2,1,0:T(8,128)(2,1)S(1)} %copy-done.3, ...), custom_call_target="tpu_custom_call" | custom-call | flops 2147483648 | bytes 2097152 | tf_op jit(solution)/shard_map/pallas_call | solution.py:108
  142.5 21.0 %all-gather.3.cloned.1.call-done.q_ref = bf16[16,128,2048]{2,1,0:T(8,128)(2,1)} async-done(((bf16[2,128,2048]{2,1,0:T(8,128)(2,1)}), bf16[16,128,2048]{2,1,0:T(8,128)(2,1)}) %all-gather.3.cloned.1.call-update) | async-done | bytes 8388624 | tf_op jit(solution)/shard_map/all_gather | solution.py:172
  163.5 3.4 copy-done
  166.8 2.2 copy-done.4
  169.0 2.2 copy-done.7
  171.2 17.0 %shard_map.76 = bf16[2,2,144,1024]{3,2,1,0:T(8,128)(2,1)} custom-call(s32[2]{0:T(128)S(1)} %iota_add_fusion.4.qsel.gsel, s32[2]{0:T(128)S(1)} %iota_add_fusion.4.qsel.gsel, s32[16]{0:T(128)S(1)} %convert_reduce_fusion.counts, s32[288]{0:T(512)S(1)} %reshape.83.ids, bf16[16,128,2048]{2,1,0:T(8,128)(2,1)S(1)} %copy-done, ...), custom_call_target="tpu_custom_call" | custom-call | flops 2147483648 | bytes 2097152 | tf_op jit(solution)/shard_map/pallas_call | solution.py:108
  188.2 17.0 %shard_map.75 = bf16[2,2,144,1024]{3,2,1,0:T(8,128)(2,1)} custom-call(s32[2]{0:T(128)S(1)} %iota_add_fusion.5.qsel.gsel, s32[2]{0:T(128)S(1)} %iota_add_fusion.5.qsel.gsel, s32[16]{0:T(128)S(1)} %convert_reduce_fusion.counts, s32[288]{0:T(512)S(1)} %reshape.83.ids, bf16[16,128,2048]{2,1,0:T(8,128)(2,1)S(1)} %copy-done, ...), custom_call_target="tpu_custom_call" | custom-call | flops 2147483648 | bytes 2097152 | tf_op jit(solution)/shard_map/pallas_call | solution.py:108
  205.3 16.3 %collective-permute-start.1 = (bf16[2,2,144,1024]{3,2,1,0:T(8,128)(2,1)}, bf16[2,2,144,1024]{3,2,1,0:T(8,128)(2,1)}, u32[]{:S(2)}, u32[]{:S(2)}) collective-permute-start(bf16[2,2,144,1024]{3,2,1,0:T(8,128)(2,1)} %shard_map.75), channel_id=1, source_target_pairs={{0,24},{2,26},{4,28},{6,30},{8,16},{10,18},{12,20},{14,22},{16,8},... | collective-permute-start | bytes 3538952 | tf_op jit(solution)/shard_map/ppermute | solution.py:196
  221.5 19.5 %shard_map.74 = bf16[2,2,144,1024]{3,2,1,0:T(8,128)(2,1)} custom-call(s32[2]{0:T(128)S(1)} %iota_add_fusion.6.qsel.gsel, s32[2]{0:T(128)S(1)} %iota_add_fusion.6.qsel.gsel, s32[16]{0:T(128)S(1)} %convert_reduce_fusion.counts, s32[288]{0:T(512)S(1)} %reshape.83.ids, bf16[16,128,2048]{2,1,0:T(8,128)(2,1)S(1)} %bitcast.84, ...), custom_call_target="tpu_custom_call" | custom-call | flops 2147483648 | bytes 2097152 | tf_op jit(solution)/shard_map/pallas_call | solution.py:108
  241.0 24.7 %collective-permute-start = (bf16[2,2,144,1024]{3,2,1,0:T(8,128)(2,1)}, bf16[2,2,144,1024]{3,2,1,0:T(8,128)(2,1)}, u32[]{:S(2)}, u32[]{:S(2)}) collective-permute-start(bf16[2,2,144,1024]{3,2,1,0:T(8,128)(2,1)} %shard_map.74), channel_id=1, source_target_pairs={{0,28},{2,30},{4,24},{6,26},{8,20},{10,22},{12,16},{14,18},{16,12}... | collective-permute-start | bytes 3538952 | tf_op jit(solution)/shard_map/ppermute | solution.py:196
  265.8 3.4 copy-done.1
  269.1 2.2 copy-done.5
  271.3 2.2 copy-done.8
  273.5 16.2 %shard_map.77 = bf16[2,2,144,1024]{3,2,1,0:T(8,128)(2,1)S(1)} custom-call(s32[2]{0:T(128)S(1)} %iota_add_fusion.3.qsel.gsel, s32[2]{0:T(128)S(1)} %iota_add_fusion.3.qsel.gsel, s32[16]{0:T(128)S(1)} %convert_reduce_fusion.counts, s32[288]{0:T(512)S(1)} %reshape.83.ids, bf16[16,128,2048]{2,1,0:T(8,128)(2,1)S(1)} %copy-done.1, ...), custom_call_target="tpu_custom_call" | custom-call | flops 2147483648 | bytes 2097152 | tf_op jit(solution)/shard_map/pallas_call | solution.py:108
  289.8 5.2 %collective-permute-done.2.rest_0_ = bf16[2,2,144,1024]{3,2,1,0:T(8,128)(2,1)S(1)} collective-permute-done((bf16[2,2,144,1024]{3,2,1,0:T(8,128)(2,1)}, bf16[2,2,144,1024]{3,2,1,0:T(8,128)(2,1)S(1)}, u32[]{:S(2)}, u32[]{:S(2)}) %collective-permute-start.2) | collective-permute-done | bytes 1179680 | tf_op jit(solution)/shard_map/ppermute | solution.py:196
  295.0 3.4 copy-done.2
  298.4 18.9 %shard_map.80 = bf16[2,2,144,1024]{3,2,1,0:T(8,128)(2,1)S(1)} custom-call(s32[2]{0:T(128)S(1)} %iota_add_fusion.qsel.gsel, s32[2]{0:T(128)S(1)} %iota_add_fusion.qsel.gsel, s32[16]{0:T(128)S(1)} %convert_reduce_fusion.counts, s32[288]{0:T(512)S(1)} %reshape.83.ids, bf16[16,128,2048]{2,1,0:T(8,128)(2,1)S(1)} %copy-done.2, ...), custom_call_target="tpu_custom_call" | custom-call | flops 2147483648 | bytes 2097152 | tf_op jit(solution)/shard_map/pallas_call | solution.py:108
  317.3 23.8 %collective-permute-start.6 = (bf16[2,2,144,1024]{3,2,1,0:T(8,128)(2,1)S(1)}, bf16[2,2,144,1024]{3,2,1,0:T(8,128)(2,1)}, u32[]{:S(2)}, u32[]{:S(2)}) collective-permute-start(bf16[2,2,144,1024]{3,2,1,0:T(8,128)(2,1)S(1)} %shard_map.80), channel_id=1, source_target_pairs={{0,4},{2,6},{4,0},{6,2},{8,12},{10,14},{12,8},{14,10},{16,20},{18,... | collective-permute-start | bytes 3538952 | tf_op jit(solution)/shard_map/ppermute | solution.py:196
  341.1 16.2 %shard_map.79 = bf16[2,2,144,1024]{3,2,1,0:T(8,128)(2,1)S(1)} custom-call(s32[2]{0:T(128)S(1)} %iota_add_fusion.1.qsel.gsel, s32[2]{0:T(128)S(1)} %iota_add_fusion.1.qsel.gsel, s32[16]{0:T(128)S(1)} %convert_reduce_fusion.counts, s32[288]{0:T(512)S(1)} %reshape.83.ids, bf16[16,128,2048]{2,1,0:T(8,128)(2,1)S(1)} %copy-done.2, ...), custom_call_target="tpu_custom_call" | custom-call | flops 2147483648 | bytes 2097152 | tf_op jit(solution)/shard_map/pallas_call | solution.py:108
  357.4 13.7 %shard_map.78 = bf16[2,2,144,1024]{3,2,1,0:T(8,128)(2,1)S(1)} custom-call(s32[2]{0:T(128)S(1)} %iota_add_fusion.2.qsel.gsel, s32[2]{0:T(128)S(1)} %iota_add_fusion.2.qsel.gsel, s32[16]{0:T(128)S(1)} %convert_reduce_fusion.counts, s32[288]{0:T(512)S(1)} %reshape.83.ids, bf16[16,128,2048]{2,1,0:T(8,128)(2,1)S(1)} %copy-done.2, ...), custom_call_target="tpu_custom_call" | custom-call | flops 2147483648 | bytes 2097152 | tf_op jit(solution)/shard_map/pallas_call | solution.py:108
  371.1 13.9 %collective-permute-start.4 = (bf16[2,2,144,1024]{3,2,1,0:T(8,128)(2,1)S(1)}, bf16[2,2,144,1024]{3,2,1,0:T(8,128)(2,1)S(1)}, u32[]{:S(2)}, u32[]{:S(2)}) collective-permute-start(bf16[2,2,144,1024]{3,2,1,0:T(8,128)(2,1)S(1)} %shard_map.78), channel_id=1, source_target_pairs={{0,12},{2,14},{4,8},{6,10},{8,4},{10,6},{12,0},{14,2},{16,28},{18,... | collective-permute-start | bytes 3538952 | tf_op jit(solution)/shard_map/ppermute | solution.py:196
  385.3 1.6 convert_element_type.30
  386.9 1.6 convert_element_type.29
  388.5 7.1 %collective-permute-done.3 = bf16[2,2,144,1024]{3,2,1,0:T(8,128)(2,1)S(1)} collective-permute-done((bf16[2,2,144,1024]{3,2,1,0:T(8,128)(2,1)S(1)}, bf16[2,2,144,1024]{3,2,1,0:T(8,128)(2,1)S(1)}, u32[]{:S(2)}, u32[]{:S(2)}) %collective-permute-start.3) | collective-permute-done | bytes 1179680 | tf_op jit(solution)/shard_map/ppermute | solution.py:196
  395.9 1.6 convert_element_type.35
  397.4 14.2 %collective-permute-done.5 = bf16[2,2,144,1024]{3,2,1,0:T(8,128)(2,1)} collective-permute-done((bf16[2,2,144,1024]{3,2,1,0:T(8,128)(2,1)S(1)}, bf16[2,2,144,1024]{3,2,1,0:T(8,128)(2,1)}, u32[]{:S(2)}, u32[]{:S(2)}) %collective-permute-start.5) | collective-permute-done | bytes 1179680 | tf_op jit(solution)/shard_map/ppermute | solution.py:196
  411.7 1.6 convert_element_type.34
  413.2 31.8 %collective-permute-done.4 = bf16[2,2,144,1024]{3,2,1,0:T(8,128)(2,1)S(1)} collective-permute-done((bf16[2,2,144,1024]{3,2,1,0:T(8,128)(2,1)S(1)}, bf16[2,2,144,1024]{3,2,1,0:T(8,128)(2,1)S(1)}, u32[]{:S(2)}, u32[]{:S(2)}) %collective-permute-start.4) | collective-permute-done | bytes 1179680 | tf_op jit(solution)/shard_map/ppermute | solution.py:196
  446.1 2.1 copy_bitcast_fusion.1
  448.2 4.6 all_to_all.47
  453.3 1.4 reduce
  456.1 16.6 %all_to_all.48 = bf16[2,2,131072]{2,1,0:T(2,128)(2,1)S(1)} all-to-all(bf16[2,2,131072]{2,1,0:T(2,128)(2,1)S(1)} %reshape.98), channel_id=1, replica_groups=mesh['dp'=16,'tensor'=2] {'tensor'}, dimensions={0} | all-to-all | bytes 2097152 | tf_op jit(solution)/shard_map/all_to_all | solution.py:133
  473.6 1.1 copy.133
  474.8 1.1 copy.124
  475.9 1.6 copy.137
  (82 shorter events, 11.6 us)
Async XLA Ops:
  6.5 1.9 copy-start.12
  6.5 2.0 copy-start.13
  6.5 156.9 %all-gather.3.cloned.1.call-start = ((), (), s32[]{:S(2)}) async-start(), calls=%async_computation.5 | async-start | bytes 9437184 | tf_op jit(solution)/shard_map/all_gather | solution.py:172
  67.0 7.8 %copy-start.14 = (s32[1,64]{1,0:T(1,128)S(1)}, s32[1,64]{1,0:T(1,128)}, u32[]{:S(2)}) copy-start(s32[1,64]{1,0:T(1,128)} %param.12) | copy-start | bytes 772
  67.0 7.8 %copy-start.15 = (s32[1,64,1]{1,2,0:T(1,128)S(1)}, s32[1,64,1]{1,2,0:T(1,128)}, u32[]{:S(2)}) copy-start(s32[1,64,1]{1,2,0:T(1,128)} %param.11) | copy-start | bytes 772
  67.0 30.4 %all-to-all-start.2 = ((bf16[2,32,2,128,256]{3,4,1,2,0:T(8,128)(2,1)}), bf16[2,32,2,128,256]{3,4,1,2,0:T(8,128)(2,1)}, u32[]{:S(2)}, u32[]{:S(2)}) async-start(bf16[2,32,2,128,256]{3,4,1,2,0:T(8,128)(2,1)} %copy.109), calls=%async_computation.2 | async-start | bytes 16777216 | tf_op jit(solution)/shard_map/all_to_all | solution.py:133
  117.7 1.7 copy-start.9
  119.5 2.2 copy-start.3
  121.7 2.2 copy-start.6
  123.8 0.9 copy-start.10
  124.8 0.7 copy-start.11
  163.4 3.4 copy-start
  166.8 2.2 copy-start.4
  169.0 2.2 copy-start.7
  171.2 50.3 %slice-start = ((s8[8388608]{0:T(1024)(128)(4,1)}), s8[4194304]{0:T(1024)(128)(4,1)S(1)}, s32[]{:S(2)}) async-start(s8[8388608]{0:T(1024)(128)(4,1)} %bitcast.83), calls=%async_computation.6 | async-start | bytes 8388608
  188.2 33.3 %slice-start.1 = ((s8[8388608]{0:T(1024)(128)(4,1)}), s8[4194304]{0:T(1024)(128)(4,1)S(1)}, s32[]{:S(2)}) async-start(s8[8388608]{0:T(1024)(128)(4,1)} %bitcast.83), calls=%async_computation.7 | async-start | bytes 8388608
  188.2 106.8 %collective-permute-start.2 = (bf16[2,2,144,1024]{3,2,1,0:T(8,128)(2,1)}, bf16[2,2,144,1024]{3,2,1,0:T(8,128)(2,1)S(1)}, u32[]{:S(2)}, u32[]{:S(2)}) collective-permute-start(bf16[2,2,144,1024]{3,2,1,0:T(8,128)(2,1)} %shard_map.76), channel_id=1, source_target_pairs={{0,20},{2,22},{4,16},{6,18},{8,28},{10,30},{12,24},{14,26},{16,4},... | collective-permute-start | bytes 3538952 | tf_op jit(solution)/shard_map/ppermute | solution.py:196
  205.3 135.9 %collective-permute-start.1 = (bf16[2,2,144,1024]{3,2,1,0:T(8,128)(2,1)}, bf16[2,2,144,1024]{3,2,1,0:T(8,128)(2,1)}, u32[]{:S(2)}, u32[]{:S(2)}) collective-permute-start(bf16[2,2,144,1024]{3,2,1,0:T(8,128)(2,1)} %shard_map.75), channel_id=1, source_target_pairs={{0,24},{2,26},{4,28},{6,30},{8,16},{10,18},{12,20},{14,22},{16,8},... | collective-permute-start | bytes 3538952 | tf_op jit(solution)/shard_map/ppermute | solution.py:196
  241.0 116.4 %collective-permute-start = (bf16[2,2,144,1024]{3,2,1,0:T(8,128)(2,1)}, bf16[2,2,144,1024]{3,2,1,0:T(8,128)(2,1)}, u32[]{:S(2)}, u32[]{:S(2)}) collective-permute-start(bf16[2,2,144,1024]{3,2,1,0:T(8,128)(2,1)} %shard_map.74), channel_id=1, source_target_pairs={{0,28},{2,30},{4,24},{6,26},{8,20},{10,22},{12,16},{14,18},{16,12}... | collective-permute-start | bytes 3538952 | tf_op jit(solution)/shard_map/ppermute | solution.py:196
  265.8 3.4 copy-start.1
  269.1 2.2 copy-start.5
  271.3 2.2 copy-start.8
  289.7 105.8 %collective-permute-start.3 = (bf16[2,2,144,1024]{3,2,1,0:T(8,128)(2,1)S(1)}, bf16[2,2,144,1024]{3,2,1,0:T(8,128)(2,1)S(1)}, u32[]{:S(2)}, u32[]{:S(2)}) collective-permute-start(bf16[2,2,144,1024]{3,2,1,0:T(8,128)(2,1)S(1)} %shard_map.77), channel_id=1, source_target_pairs={{0,16},{2,18},{4,20},{6,22},{8,24},{10,26},{12,28},{14,30},{16,0},... | collective-permute-start | bytes 3538952 | tf_op jit(solution)/shard_map/ppermute | solution.py:196
  295.0 3.4 copy-start.2
  317.3 78.6 %collective-permute-start.6 = (bf16[2,2,144,1024]{3,2,1,0:T(8,128)(2,1)S(1)}, bf16[2,2,144,1024]{3,2,1,0:T(8,128)(2,1)}, u32[]{:S(2)}, u32[]{:S(2)}) collective-permute-start(bf16[2,2,144,1024]{3,2,1,0:T(8,128)(2,1)S(1)} %shard_map.80), channel_id=1, source_target_pairs={{0,4},{2,6},{4,0},{6,2},{8,12},{10,14},{12,8},{14,10},{16,20},{18,... | collective-permute-start | bytes 3538952 | tf_op jit(solution)/shard_map/ppermute | solution.py:196
  357.3 54.4 %collective-permute-start.5 = (bf16[2,2,144,1024]{3,2,1,0:T(8,128)(2,1)S(1)}, bf16[2,2,144,1024]{3,2,1,0:T(8,128)(2,1)}, u32[]{:S(2)}, u32[]{:S(2)}) collective-permute-start(bf16[2,2,144,1024]{3,2,1,0:T(8,128)(2,1)S(1)} %shard_map.79), channel_id=1, source_target_pairs={{0,8},{2,10},{4,12},{6,14},{8,0},{10,2},{12,4},{14,6},{16,24},{18,... | collective-permute-start | bytes 3538952 | tf_op jit(solution)/shard_map/ppermute | solution.py:196
  371.1 73.9 %collective-permute-start.4 = (bf16[2,2,144,1024]{3,2,1,0:T(8,128)(2,1)S(1)}, bf16[2,2,144,1024]{3,2,1,0:T(8,128)(2,1)S(1)}, u32[]{:S(2)}, u32[]{:S(2)}) collective-permute-start(bf16[2,2,144,1024]{3,2,1,0:T(8,128)(2,1)S(1)} %shard_map.78), channel_id=1, source_target_pairs={{0,12},{2,14},{4,8},{6,10},{8,4},{10,6},{12,0},{14,2},{16,28},{18,... | collective-permute-start | bytes 3538952 | tf_op jit(solution)/shard_map/ppermute | solution.py:196
Sparse Core Ops, SparseCore 0:
  38.0 125.4 all-gather.2

commit v3 on v2

--- a/solution.py
+++ b/solution.py
@@ -20,23 +20,18 @@
 def attend_kernel(width, fresh, qsel, gsel, counts, ids, q_ref, k_ref, vt_ref, *rest):
     if fresh:
         kf_ref, vf_ref, *rest = rest
-    o_ref, q_t, acc = rest[-3:]
+    o_ref, acc = rest[-2:]
     i = pl.program_id(0)
     g = gsel[i]
     n = counts[g]
     heads = o_ref.shape[1]
     tiles = [(c, j) for c in range(heads) for j in range(ROWS // STEP)]
 
-    for c in range(heads):
-        for h in range(PER_KV):
-            at = (c * PER_KV + h) * HD
-            q_t[c, :, h * 128 : (h + 1) * 128] = q_ref[0, :, at : at + HD].T
-
     def fold(keys, vals_t, mask, second, carry):
         out = []
         for (c, j), (top, total) in zip(tiles, carry):
             cols = pl.ds(j * STEP, STEP)
-            s = jnp.dot(keys[c], q_t[c, :, cols], preferred_element_type=jnp.float32)
+            s = jnp.dot(keys[c], q_ref[0, c, :, cols], preferred_element_type=jnp.float32)
             if mask is not None:
                 s = jnp.where(mask, s, LOW)
             here = jnp.max(s[:128], axis=0, keepdims=True)
@@ -87,7 +82,8 @@
         total = jnp.sum(total, axis=0, keepdims=True)
         some = total > 0.0
         safe = jnp.where(some, total, 1.0)
-        o_ref[0, c, :HD, cols] = (acc[c, :, cols] / safe).astype(o_ref.dtype)
+        part = 1.0 / safe
+        o_ref[0, c, :HD, cols] = (acc[c, :, cols] * part).astype(o_ref.dtype)
         left = jnp.where(some, top + jnp.log2(safe), LOW)
         row = lax.broadcasted_iota(jnp.int32, (EXTRA, STEP), 0)
         terms = jnp.zeros((EXTRA, STEP), jnp.float32)
@@ -110,12 +106,11 @@
         grid_spec=pltpu.PrefetchScalarGridSpec(
             num_scalar_prefetch=4,
             grid=(count,),
-            in_specs=[pl.BlockSpec((1,) + q.shape[1:], lambda i, qs, *_: (qs[i], 0, 0))]
+            in_specs=[pl.BlockSpec((1,) + q.shape[1:], lambda i, qs, *_: (qs[i], 0, 0, 0))]
             + [pl.BlockSpec(memory_space=pltpu.VMEM)] * (2 + len(extra))
             + [pl.BlockSpec(memory_space=pl.ANY)] * len(behind),
             out_specs=pl.BlockSpec((1, heads, HD + EXTRA, ROWS), lambda i, *_: (i, 0, 0, 0)),
             scratch_shapes=[
-                pltpu.VMEM((heads, HD, ROWS), jnp.bfloat16),
                 pltpu.VMEM((heads, HD, ROWS), jnp.float32),
             ],
         ),
@@ -168,39 +163,59 @@
     turn = turn.reshape(new, span, -1).transpose(1, 0, 2)
     if span > 1:
         turn = exchange(turn, "dp", mates)
-    q = turn[:, :, :q_cols]
-    q_all = lax.all_gather(q, "dp", axis=0, tiled=True, axis_index_groups=peers)
-    fresh = turn[:, :, q_cols:].reshape(span, new, 2, heads, HD)
-    k_fresh = fresh[:, :, 0].transpose(0, 2, 1, 3)
-    v_fresh = fresh[:, :, 1].transpose(0, 2, 3, 1)
+    q = turn[:, :, :q_cols].reshape(span, new, heads, PER_KV, HD).transpose(2, 0, 4, 3, 1)
+    q = q.reshape(heads, span, 1, HD, PER_KV * new)
+    q_all = [
+        lax.all_gather(q[c], "dp", axis=0, tiled=True, axis_index_groups=peers)
+        for c in range(heads)
+    ]
+    fresh = turn[:, :, q_cols:].reshape(span, new, 2, heads, 1, HD)
+    k_fresh = fresh[:, :, 0].transpose(2, 0, 3, 1, 4)
+    v_fresh = fresh[:, :, 1].transpose(2, 0, 3, 4, 1)
 
     halves = hist_kv.reshape(pool, block, 2, span, kv_cols).transpose(3, 0, 2, 1, 4)
     if span > 1:
         halves = exchange(halves, "dp", mates)
-    halves = halves.reshape(span * pool, 2, block, heads, HD)
-    keys = halves[:, 0].transpose(0, 2, 1, 3)
-    vals_t = halves[:, 1].transpose(0, 2, 3, 1)
+    halves = halves.reshape(span * pool, 2, block, heads, 1, HD)
+    keys = halves[:, 0].transpose(2, 0, 3, 1, 4)
+    vals_t = halves[:, 1].transpose(2, 0, 3, 4, 1)
 
     core = jnp.arange(span, dtype=jnp.int32)
-    own = attend(core, unit * span + core, counts, ids, q, keys, vals_t, (k_fresh, v_fresh))
-    arrived, sent = [own], []
     apart = list(range(units - 1, 0, -1))
     per = max(1, units // 8)
-    for at in range(0, len(apart), per):
-        some = apart[at : at + per]
-        sel = jnp.concatenate([(unit ^ r) * span + core for r in some])
-        after = own if len(sent) < 4 else sent[-4]
-        part = attend(sel, sel, counts, ids, q_all, keys, vals_t, after=after)
-        for k, r in enumerate(some):
-            to = [(u * span + c, (u ^ r) * span + c) for u in range(units) for c in range(span)]
-            arrived.append(lax.ppermute(part[k * span : (k + 1) * span], "dp", to))
-        sent.append(arrived[-1])
-    arrived = [x.astype(jnp.float32) for x in arrived]
-    lses = [x[:, :, HD] + x[:, :, HD + 1] + x[:, :, HD + 2] for x in arrived]
-    top = functools.reduce(jnp.maximum, lses)
-    scales = [jnp.exp2(lse - top) for lse in lses]
-    total = sum(scales)
-    result = sum(x[:, :, :HD] * (w / total)[:, :, None, :] for x, w in zip(arrived, scales))
+    results, sent = [], []
+    arrived = [
+        [
+            attend(
+                core, unit * span + core, counts, ids, q[c], keys[c], vals_t[c],
+                (k_fresh[c], v_fresh[c]),
+            )
+        ]
+        for c in range(heads)
+    ]
+    for c in range(heads):
+        for at in range(0, len(apart), per):
+            some = apart[at : at + per]
+            sel = jnp.concatenate([(unit ^ r) * span + core for r in some])
+            after = arrived[c][0] if len(sent) < 4 else sent[-4]
+            part = attend(sel, sel, counts, ids, q_all[c], keys[c], vals_t[c], after=after)
+            for k, r in enumerate(some):
+                to = [(u * span + i, (u ^ r) * span + i) for u in range(units) for i in range(span)]
+                arrived[c].append(lax.ppermute(part[k * span : (k + 1) * span], "dp", to))
+            sent.append(arrived[c][-1])
+    for c in range(heads):
+        got = [x[:, 0] for x in arrived[c]]
+        lses = [jnp.sum(x[:, HD : HD + 3].astype(jnp.float32), axis=1) for x in got]
+        top = functools.reduce(jnp.maximum, lses)
+        scales = [jnp.exp2(lse - top) for lse in lses]
+        total = sum(scales)
+        results.append(
+            sum(
+                x[:, :HD].astype(jnp.float32) * (w / total)[:, None, :]
+                for x, w in zip(got, scales)
+            )
+        )
+    result = jnp.stack(results, axis=1)
     result = result.astype(jnp.bfloat16)
     result = result.reshape(span, heads, HD, PER_KV, new).transpose(0, 4, 1, 3, 2)
     result = result.reshape(span, new, q_cols)

time: 487 us -> 511 us (1.049)
  starting transfers between devices: 86 us -> 128 us
  waiting for transfers between devices: 79.4 us -> 50.3 us
  Pallas kernels: 136 us -> 152 us
  local copies, waits for them, and re-layouts: 87.5 us -> 80.6 us
    ppermute x7 -> x14, starting transfers between devices: 78.9 us -> 121 us  [local(): arrived[c].append(lax.ppermute(part[k * span:(k + 1) * span], 'dp', to))]
    all_gather x1 -> x2, waiting for transfers between devices: 21 us -> 0.02 us  [local(): lax.all_gather(q[c], 'dp', axis=0, tiled=True, axis_index_groups=peers)]
    pallas_call x8 -> x16, Pallas kernels: 136 us -> 152 us  [attend(): pl.pallas_call(functools.partial(attend_kernel, width, fresh is not None)...]
    transpose x3 -> x1, local copies, waits for them, and re-layouts: 13.3 us -> 0.13 us  [local(): turn = turn.reshape(new, span, -1).transpose(1, 0, 2)]
    ppermute x7 -> x14, waiting for transfers between devices: 58.4 us -> 50.3 us  [local(): arrived[c].append(lax.ppermute(part[k * span:(k + 1) * span], 'dp', to))]
    all_to_all x2 -> x1, local copies, waits for them, and re-layouts: 8.88 us -> 1.09 us  [exchange(): lax.all_to_all(x, axis, split_axis=split, concat_axis=concat, tiled=True,...]
    squeeze x0 -> x4, local copies, waits for them, and re-layouts: none -> 7.76 us  [the longest x1 5.7 us: local(): vals_t[c]]
    convert_element_type x7 -> x0, other arithmetic: 7.06 us -> none  [local(): arrived = [x.astype(jnp.float32) for x in arrived]]
  transfers between devices with their start and end apart: 9 -> 17, of which waited for: 5 -> 6; matrix products, arithmetic and copies ran while one was open for 12% -> 11% of each run, Pallas kernels for 24% -> 30%
where the time goes in v3:
time: 511 us; the launch traced here: 503 us
  Pallas kernels  152 us (30%)
  starting transfers between devices  128 us (25%)
  local copies, waits for them, and re-layouts  80.6 us (16%)
  blocking collectives  68.5 us (13%)
  waiting for transfers between devices  50.3 us (10%)
  between operations  14.8 us (3%)
  other arithmetic  9.21 us (2%)
    pallas_call x16, Pallas kernels, attend(): pl.pallas_call(functools.partial(attend_kernel, width, fresh is not None)...  152 us
    ppermute x14, starting transfers between devices, local(): arrived[c].append(lax.ppermute(part[k * span:(k + 1) * span], 'dp', to))  121 us
    unnamed x72, local copies, waits for them, and re-layouts  52.7 us
    ppermute x14, waiting for transfers between devices, local(): arrived[c].append(lax.ppermute(part[k * span:(k + 1) * span], 'dp', to))  50.3 us
    all_to_all x4, blocking collectives, exchange(): lax.all_to_all(x, axis, split_axis=split, concat_axis=concat, tiled=True,...  46.5 us
    all_gather x1, blocking collectives, local(): code = lax.all_gather(code, 'dp', axis=0, tiled=True)  22 us
  transfers between devices with their start and end apart: 17, of which 6 were waited for; matrix products, arithmetic and copies ran while one was open for 11% of the time, Pallas kernels for 30%

profile of v3, /device:TPU:0, one launch (start us, length us, event | category | flops | bytes accessed | tf_op | source)
XLA Modules:
  0.0 503.4 jit_solution(3459416464639474532)
XLA Ops:
  6.5 1.9 reshape.452
  10.4 20.4 %all_to_all.45 = bf16[64,2,5120]{2,0,1:T(8,128)(2,1)S(1)} all-to-all(bf16[64,2,5120]{2,0,1:T(8,128)(2,1)S(1)} %copy.269), channel_id=1, replica_groups=mesh['dp'=16,'tensor'=2] {'tensor'}, dimensions={1} | all-to-all | bytes 2621440 | tf_op jit(solution)/shard_map/all_to_all | solution.py:128
  31.9 4.8 all_to_all.46
  41.6 21.2 %copy.273 = bf16[32,128,2,512]{1,3,2,0:T(8,128)(2,1)} copy(bf16[32,128,2,512]{3,2,1,0:T(2,128)(2,1)} %param.10) | data formatting | bytes 16777216 | tf_op args[3]
  62.8 7.7 %copy.274 = bf16[2,32,2,128,256]{3,4,2,1,0:T(8,128)(2,1)} copy(bf16[2,32,2,128,256]{3,4,0,2,1:T(8,128)(2,1)} %bitcast.162) | data formatting | bytes 16777216 | tf_op jit(solution)/shard_map/transpose | solution.py:176
  70.6 7.2 %all-to-all-start.2 = ((bf16[2,32,2,128,256]{3,4,2,1,0:T(8,128)(2,1)}), bf16[2,32,2,128,256]{3,4,2,1,0:T(8,128)(2,1)}, u32[]{:S(2)}, u32[]{:S(2)}) async-start(bf16[2,32,2,128,256]{3,4,2,1,0:T(8,128)(2,1)} %copy.274), calls=%async_computation.2 | async-start | bytes 16777216 | tf_op jit(solution)/shard_map/all_to_all | solution.py:128
  78.5 22.0 %all-gather = s32[16,1,64]{2,1,0:T(1,128)S(1)} all-gather(s32[1,1,64]{2,1,0:T(1,128)S(1)} %fusion.20), channel_id=1, replica_groups=mesh['dp'=16,'tensor'=2] {'dp'}, dimensions={0}, use_global_device_ids=true | all-gather | bytes 4352 | tf_op jit(solution)/shard_map/all_gather | solution.py:152
  101.4 5.2 %fusion.38 = (bf16[64,1,128,2,1,128]{2,5,3,1,0,4:T(8,128)(2,1)S(1)}, bf16[64,1,128,2,1,128]{2,5,3,1,0,4:T(8,128)(2,1)}) fusion(bf16[64,2,128,2,1,128]{2,5,3,1,0,4:T(8,128)(2,1)} %bitcast.11), kind=kLoop, calls=%fused_computation.109 | loop fusion | bytes 16777216 | tf_op jit(solution)/shard_map/slice | solution.py:181
  106.6 2.2 copy.335
  108.9 6.4 %copy.325 = bf16[64,1,128,2,1,128]{5,2,0,3,4,1:T(8,128)(2,1)} copy(bf16[64,1,128,2,1,128]{2,5,3,1,0,4:T(8,128)(2,1)} %get-tuple-element.14) | data formatting | bytes 8388608
  115.5 5.7 %slice_bitcast_fusion.2 = (bf16[64,1,128,128]{3,2,1,0:T(8,128)(2,1)}, bf16[64,1,128,128]{3,2,1,0:T(8,128)(2,1)S(1)}, bf16[64,1,128,128]{3,2,1,0:T(8,128)(2,1)}, bf16[64,1,128,128]{3,2,1,0:T(8,128)(2,1)}) fusion(bf16[2,64,1,128,128]{4,3,1,2,0:T(8,128)(2,1)} %bitcast.163, bf16[2,64,1,128,128]{4,3,1,2,0:T(8,128)(2,1)} %bitcast.164), kind=kLoop, calls=%fused_computation.3 | loop fusion | bytes 16777216 | tf_op jit(solution)/shard_map/squeeze | solution.py:190
  121.6 1.8 copy-done.6
  123.3 1.7 copy-done.8
  126.1 10.8 %shard_map.73.rest_0_ = f32[2,1,144,1024]{3,2,1,0:T(8,128)S(1)} custom-call(s32[2]{0:T(128)S(1)} %iota.29.qsel, s32[2]{0:T(128)S(1)} %iota_add_fusion.7.gsel, s32[16]{0:T(128)S(1)} %convert_reduce_fusion.14.counts, s32[288]{0:T(512)S(1)} %reshape.451.ids, bf16[2,1,128,1024]{3,2,1,0:T(8,128)(2,1)S(1)} %copy-done.12, bf16[64,1,128,128]{3,2,1,0:T(8,128)(2,1)S(1)} %copy-done.8, ...), custom_call_target="tpu_custom_call" | custom-call | flops 1073741824 | bytes 1048576 | tf_op jit(solution)/shard_map/pallas_call | solution.py:104
  136.9 2.2 copy-done.2
  139.1 1.6 copy-done.7
  140.7 1.6 copy-done.9
  142.3 11.2 %shard_map.76 = bf16[2,1,144,1024]{3,2,1,0:T(8,128)(2,1)S(1)} custom-call(s32[2]{0:T(128)S(1)} %iota_add_fusion.4.qsel.gsel, s32[2]{0:T(128)S(1)} %iota_add_fusion.4.qsel.gsel, s32[16]{0:T(128)S(1)} %convert_reduce_fusion.14.counts, s32[288]{0:T(512)S(1)} %reshape.451.ids, bf16[16,1,128,1024]{3,2,1,0:T(8,128)(2,1)S(1)} %copy-done.2, ...), custom_call_target="tpu_custom_call" | custom-call | flops 1073741824 | bytes 1048576 | tf_op jit(solution)/shard_map/pallas_call | solution.py:104
  153.6 4.7 shard_map.74
  158.3 29.1 %collective-permute-start = (bf16[2,1,144,1024]{3,2,0,1:T(8,128)(2,1)S(1)}, bf16[2,1,144,1024]{3,2,0,1:T(8,128)(2,1)S(1)}, u32[]{:S(2)}, u32[]{:S(2)}) collective-permute-start(bf16[2,1,144,1024]{3,2,0,1:T(8,128)(2,1)S(1)} %bitcast.158), channel_id=1, source_target_pairs={{0,28},{2,30},{4,24},{6,26},{8,20},{10,22},{12,16},{14,18},{16,12}... | collective-permute-start | bytes 1769480 | tf_op jit(solution)/shard_map/ppermute | solution.py:204
  187.4 8.6 %shard_map.77 = bf16[2,1,144,1024]{3,2,1,0:T(8,128)(2,1)S(1)} custom-call(s32[2]{0:T(128)S(1)} %iota_add_fusion.3.qsel.gsel, s32[2]{0:T(128)S(1)} %iota_add_fusion.3.qsel.gsel, s32[16]{0:T(128)S(1)} %convert_reduce_fusion.14.counts, s32[288]{0:T(512)S(1)} %reshape.451.ids, bf16[16,1,128,1024]{3,2,1,0:T(8,128)(2,1)S(1)} %copy-done.2, ...), custom_call_target="tpu_custom_call" | custom-call | flops 1073741824 | bytes 1048576 | tf_op jit(solution)/shard_map/pallas_call | solution.py:104
  196.1 9.9 %shard_map.75 = bf16[2,1,144,1024]{3,2,1,0:T(8,128)(2,1)S(1)} custom-call(s32[2]{0:T(128)S(1)} %iota_add_fusion.5.qsel.gsel, s32[2]{0:T(128)S(1)} %iota_add_fusion.5.qsel.gsel, s32[16]{0:T(128)S(1)} %convert_reduce_fusion.14.counts, s32[288]{0:T(512)S(1)} %reshape.451.ids, bf16[16,1,128,1024]{3,2,1,0:T(8,128)(2,1)S(1)} %copy-done.3, ...), custom_call_target="tpu_custom_call" | custom-call | flops 1073741824 | bytes 1048576 | tf_op jit(solution)/shard_map/pallas_call | solution.py:104
  206.1 10.8 %shard_map.81 = f32[2,1,144,1024]{3,2,1,0:T(8,128)S(1)} custom-call(s32[2]{0:T(128)S(1)} %iota.39.qsel, s32[2]{0:T(128)S(1)} %iota_add_fusion.7.gsel, s32[16]{0:T(128)S(1)} %convert_reduce_fusion.14.counts, s32[288]{0:T(512)S(1)} %reshape.451.ids, bf16[2,1,128,1024]{3,2,1,0:T(8,128)(2,1)S(1)} %copy-done.11, bf16[64,1,128,128]{3,2,1,0:T(8,128)(2,1)S(1)} %copy-done.4, ...), custom_call_target="tpu_custom_call" | custom-call | flops 1073741824 | bytes 1048576 | tf_op jit(solution)/shard_map/pallas_call | solution.py:104
  216.9 31.8 %collective-permute-done.2 = bf16[2,1,144,1024]{3,2,0,1:T(8,128)(2,1)S(1)} collective-permute-done((bf16[2,1,144,1024]{3,2,0,1:T(8,128)(2,1)S(1)}, bf16[2,1,144,1024]{3,2,0,1:T(8,128)(2,1)S(1)}, u32[]{:S(2)}, u32[]{:S(2)}) %collective-permute-start.2) | collective-permute-done | bytes 589856 | tf_op jit(solution)/shard_map/ppermute | solution.py:204
  248.7 11.9 %shard_map.80 = bf16[2,1,144,1024]{3,2,1,0:T(8,128)(2,1)} custom-call(s32[2]{0:T(128)S(1)} %iota_add_fusion.qsel.gsel, s32[2]{0:T(128)S(1)} %iota_add_fusion.qsel.gsel, s32[16]{0:T(128)S(1)} %convert_reduce_fusion.14.counts, s32[288]{0:T(512)S(1)} %reshape.451.ids, bf16[16,1,128,1024]{3,2,1,0:T(8,128)(2,1)S(1)} %copy-done.3, ...), custom_call_target="tpu_custom_call" | custom-call | flops 1073741824 | bytes 1048576 | tf_op jit(solution)/shard_map/pallas_call | solution.py:104
  260.7 9.3 %shard_map.78 = bf16[2,1,144,1024]{3,2,1,0:T(8,128)(2,1)} custom-call(s32[2]{0:T(128)S(1)} %iota_add_fusion.2.qsel.gsel, s32[2]{0:T(128)S(1)} %iota_add_fusion.2.qsel.gsel, s32[16]{0:T(128)S(1)} %convert_reduce_fusion.14.counts, s32[288]{0:T(512)S(1)} %reshape.451.ids, bf16[16,1,128,1024]{3,2,1,0:T(8,128)(2,1)S(1)} %copy-done.3, ...), custom_call_target="tpu_custom_call" | custom-call | flops 1073741824 | bytes 1048576 | tf_op jit(solution)/shard_map/pallas_call | solution.py:104
  270.0 5.7 %collective-permute-start.4 = (bf16[2,1,144,1024]{3,2,0,1:T(8,128)(2,1)}, bf16[2,1,144,1024]{3,2,0,1:T(8,128)(2,1)}, u32[]{:S(2)}, u32[]{:S(2)}) collective-permute-start(bf16[2,1,144,1024]{3,2,0,1:T(8,128)(2,1)} %bitcast.41), channel_id=1, source_target_pairs={{0,12},{2,14},{4,8},{6,10},{8,4},{10,6},{12,0},{14,2},{16,28},{18,... | collective-permute-start | bytes 1769480 | tf_op jit(solution)/shard_map/ppermute | solution.py:204
  276.6 10.6 %shard_map.79 = bf16[2,1,144,1024]{3,2,1,0:T(8,128)(2,1)} custom-call(s32[2]{0:T(128)S(1)} %iota_add_fusion.1.qsel.gsel, s32[2]{0:T(128)S(1)} %iota_add_fusion.1.qsel.gsel, s32[16]{0:T(128)S(1)} %convert_reduce_fusion.14.counts, s32[288]{0:T(512)S(1)} %reshape.451.ids, bf16[16,1,128,1024]{3,2,1,0:T(8,128)(2,1)S(1)} %copy-done.3, ...), custom_call_target="tpu_custom_call" | custom-call | flops 1073741824 | bytes 1048576 | tf_op jit(solution)/shard_map/pallas_call | solution.py:104
  287.2 9.0 %collective-permute-start.5 = (bf16[2,1,144,1024]{3,2,0,1:T(8,128)(2,1)}, bf16[2,1,144,1024]{3,2,0,1:T(8,128)(2,1)}, u32[]{:S(2)}, u32[]{:S(2)}) collective-permute-start(bf16[2,1,144,1024]{3,2,0,1:T(8,128)(2,1)} %bitcast.44), channel_id=1, source_target_pairs={{0,8},{2,10},{4,12},{6,14},{8,0},{10,2},{12,4},{14,6},{16,24},{18,... | collective-permute-start | bytes 1769480 | tf_op jit(solution)/shard_map/ppermute | solution.py:204
  296.1 2.2 copy-done
  301.0 4.9 shard_map.82
  305.9 35.2 %collective-permute-start.7 = (bf16[2,1,144,1024]{3,2,0,1:T(8,128)(2,1)S(1)}, bf16[2,1,144,1024]{3,2,0,1:T(8,128)(2,1)S(1)}, u32[]{:S(2)}, u32[]{:S(2)}) collective-permute-start(bf16[2,1,144,1024]{3,2,0,1:T(8,128)(2,1)S(1)} %bitcast.161), channel_id=1, source_target_pairs={{0,28},{2,30},{4,24},{6,26},{8,20},{10,22},{12,16},{14,18},{16,12}... | collective-permute-start | bytes 1769480 | tf_op jit(solution)/shard_map/ppermute | solution.py:204
  341.2 8.6 %shard_map.85 = bf16[2,1,144,1024]{3,2,1,0:T(8,128)(2,1)S(1)} custom-call(s32[2]{0:T(128)S(1)} %iota_add_fusion.3.qsel.gsel, s32[2]{0:T(128)S(1)} %iota_add_fusion.3.qsel.gsel, s32[16]{0:T(128)S(1)} %convert_reduce_fusion.14.counts, s32[288]{0:T(512)S(1)} %reshape.451.ids, bf16[16,1,128,1024]{3,2,1,0:T(8,128)(2,1)S(1)} %copy-done, ...), custom_call_target="tpu_custom_call" | custom-call | flops 1073741824 | bytes 1048576 | tf_op jit(solution)/shard_map/pallas_call | solution.py:104
  352.3 2.6 collective-permute-done.7
  354.9 8.6 %shard_map.86 = bf16[2,1,144,1024]{3,2,1,0:T(8,128)(2,1)S(1)} custom-call(s32[2]{0:T(128)S(1)} %iota_add_fusion.2.qsel.gsel, s32[2]{0:T(128)S(1)} %iota_add_fusion.2.qsel.gsel, s32[16]{0:T(128)S(1)} %convert_reduce_fusion.14.counts, s32[288]{0:T(512)S(1)} %reshape.451.ids, bf16[16,1,128,1024]{3,2,1,0:T(8,128)(2,1)S(1)} %copy-done, ...), custom_call_target="tpu_custom_call" | custom-call | flops 1073741824 | bytes 1048576 | tf_op jit(solution)/shard_map/pallas_call | solution.py:104
  363.5 14.2 %collective-permute-start.11 = (bf16[2,1,144,1024]{3,2,0,1:T(8,128)(2,1)S(1)}, bf16[2,1,144,1024]{3,2,0,1:T(8,128)(2,1)S(1)}, u32[]{:S(2)}, u32[]{:S(2)}) collective-permute-start(bf16[2,1,144,1024]{3,2,0,1:T(8,128)(2,1)S(1)} %bitcast.153), channel_id=1, source_target_pairs={{0,12},{2,14},{4,8},{6,10},{8,4},{10,6},{12,0},{14,2},{16,28},{18,... | collective-permute-start | bytes 1769480 | tf_op jit(solution)/shard_map/ppermute | solution.py:204
  377.6 9.9 %shard_map.83 = bf16[2,1,144,1024]{3,2,1,0:T(8,128)(2,1)S(1)} custom-call(s32[2]{0:T(128)S(1)} %iota_add_fusion.5.qsel.gsel, s32[2]{0:T(128)S(1)} %iota_add_fusion.5.qsel.gsel, s32[16]{0:T(128)S(1)} %convert_reduce_fusion.14.counts, s32[288]{0:T(512)S(1)} %reshape.451.ids, bf16[16,1,128,1024]{3,2,1,0:T(8,128)(2,1)S(1)} %copy-done.1, ...), custom_call_target="tpu_custom_call" | custom-call | flops 1073741824 | bytes 1048576 | tf_op jit(solution)/shard_map/pallas_call | solution.py:104
  387.5 3.7 collective-permute-start.8
  391.2 11.2 %shard_map.84 = bf16[2,1,144,1024]{3,2,1,0:T(8,128)(2,1)S(1)} custom-call(s32[2]{0:T(128)S(1)} %iota_add_fusion.4.qsel.gsel, s32[2]{0:T(128)S(1)} %iota_add_fusion.4.qsel.gsel, s32[16]{0:T(128)S(1)} %convert_reduce_fusion.14.counts, s32[288]{0:T(512)S(1)} %reshape.451.ids, bf16[16,1,128,1024]{3,2,1,0:T(8,128)(2,1)S(1)} %copy-done.1, ...), custom_call_target="tpu_custom_call" | custom-call | flops 1073741824 | bytes 1048576 | tf_op jit(solution)/shard_map/pallas_call | solution.py:104
  402.6 2.3 fusion.15
  405.5 9.9 %shard_map.87 = bf16[2,1,144,1024]{3,2,1,0:T(8,128)(2,1)S(1)} custom-call(s32[2]{0:T(128)S(1)} %iota_add_fusion.1.qsel.gsel, s32[2]{0:T(128)S(1)} %iota_add_fusion.1.qsel.gsel, s32[16]{0:T(128)S(1)} %convert_reduce_fusion.14.counts, s32[288]{0:T(512)S(1)} %reshape.451.ids, bf16[16,1,128,1024]{3,2,1,0:T(8,128)(2,1)S(1)} %copy-done.1, ...), custom_call_target="tpu_custom_call" | custom-call | flops 1073741824 | bytes 1048576 | tf_op jit(solution)/shard_map/pallas_call | solution.py:104
  415.4 23.4 %collective-permute-start.12 = (bf16[2,1,144,1024]{3,2,0,1:T(8,128)(2,1)S(1)}, bf16[2,1,144,1024]{3,2,0,1:T(8,128)(2,1)S(1)}, u32[]{:S(2)}, u32[]{:S(2)}) collective-permute-start(bf16[2,1,144,1024]{3,2,0,1:T(8,128)(2,1)S(1)} %bitcast.157), channel_id=1, source_target_pairs={{0,8},{2,10},{4,12},{6,14},{8,0},{10,2},{12,4},{14,6},{16,24},{18,... | collective-permute-start | bytes 1769480 | tf_op jit(solution)/shard_map/ppermute | solution.py:204
  438.9 2.7 collective-permute-done.9.rest_0_
  441.5 11.2 %shard_map.88 = bf16[2,1,144,1024]{3,2,1,0:T(8,128)(2,1)S(1)} custom-call(s32[2]{0:T(128)S(1)} %iota_add_fusion.qsel.gsel, s32[2]{0:T(128)S(1)} %iota_add_fusion.qsel.gsel, s32[16]{0:T(128)S(1)} %convert_reduce_fusion.14.counts, s32[288]{0:T(512)S(1)} %reshape.451.ids, bf16[16,1,128,1024]{3,2,1,0:T(8,128)(2,1)S(1)} %copy-done.1, ...), custom_call_target="tpu_custom_call" | custom-call | flops 1073741824 | bytes 1048576 | tf_op jit(solution)/shard_map/pallas_call | solution.py:104
  453.2 1.6 collective-permute-done.12
  454.9 11.0 %collective-permute-done.13 = bf16[2,1,144,1024]{3,2,0,1:T(8,128)(2,1)S(1)} collective-permute-done((bf16[2,1,144,1024]{3,2,0,1:T(8,128)(2,1)S(1)}, bf16[2,1,144,1024]{3,2,0,1:T(8,128)(2,1)S(1)}, u32[]{:S(2)}, u32[]{:S(2)}) %collective-permute-start.13) | collective-permute-done | bytes 589856 | tf_op jit(solution)/shard_map/ppermute | solution.py:204
  467.3 4.6 all_to_all.47
  475.2 16.7 %all_to_all.48 = bf16[2,2,131072]{2,1,0:T(2,128)(2,1)S(1)} all-to-all(bf16[2,2,131072]{2,1,0:T(2,128)(2,1)S(1)} %reshape.466), channel_id=1, replica_groups=mesh['dp'=16,'tensor'=2] {'tensor'}, dimensions={0} | all-to-all | bytes 2097152 | tf_op jit(solution)/shard_map/all_to_all | solution.py:128
  (148 shorter events, 27.2 us)
Async XLA Ops:
  6.5 1.9 copy-start.25
  6.5 2.0 copy-start.26
  6.5 130.3 %all-gather.4.cloned.1.call-start = ((), (), s32[]{:S(2)}) async-start(), calls=%async_computation.5 | async-start | bytes 4718592 | tf_op jit(solution)/shard_map/all_gather | solution.py:169
  36.7 1.2 copy-start.24
  40.2 255.9 %all-gather.6.cloned.1.call-start = ((), (), s32[]{:S(2)}) async-start(), calls=%async_computation.6 | async-start | bytes 4718592 | tf_op jit(solution)/shard_map/all_gather | solution.py:169
  70.6 7.9 %copy-start.27 = (s32[1,64]{1,0:T(1,128)S(1)}, s32[1,64]{1,0:T(1,128)}, u32[]{:S(2)}) copy-start(s32[1,64]{1,0:T(1,128)} %param.12) | copy-start | bytes 772
  70.6 7.9 %copy-start.28 = (s32[1,64,1]{1,2,0:T(1,128)S(1)}, s32[1,64,1]{1,2,0:T(1,128)}, u32[]{:S(2)}) copy-start(s32[1,64,1]{1,2,0:T(1,128)} %param.11) | copy-start | bytes 772
  70.6 30.8 %all-to-all-start.2 = ((bf16[2,32,2,128,256]{3,4,2,1,0:T(8,128)(2,1)}), bf16[2,32,2,128,256]{3,4,2,1,0:T(8,128)(2,1)}, u32[]{:S(2)}, u32[]{:S(2)}) async-start(bf16[2,32,2,128,256]{3,4,2,1,0:T(8,128)(2,1)} %copy.274), calls=%async_computation.2 | async-start | bytes 16777216 | tf_op jit(solution)/shard_map/all_to_all | solution.py:128
  115.5 5.7 %slice-start = ((bf16[2,128,2560]{2,1,0:T(8,128)(2,1)}), bf16[2,128,512]{2,1,0:T(8,128)(2,1)S(1)}, s32[]{:S(2)}) async-start(bf16[2,128,2560]{2,1,0:T(8,128)(2,1)} %copy-done.24), calls=%async_computation.7 | async-start | bytes 524288 | tf_op jit(solution)/shard_map/slice | solution.py:172
  121.6 1.8 copy-start.6
  123.3 1.7 copy-start.8
  125.0 1.0 copy-start.12
  136.9 2.2 copy-start.2
  139.1 1.6 copy-start.7
  140.7 1.6 copy-start.9
  153.5 95.2 %collective-permute-start.2 = (bf16[2,1,144,1024]{3,2,0,1:T(8,128)(2,1)S(1)}, bf16[2,1,144,1024]{3,2,0,1:T(8,128)(2,1)S(1)}, u32[]{:S(2)}, u32[]{:S(2)}) collective-permute-start(bf16[2,1,144,1024]{3,2,0,1:T(8,128)(2,1)S(1)} %bitcast.160), channel_id=1, source_target_pairs={{0,20},{2,22},{4,16},{6,18},{8,28},{10,30},{12,24},{14,26},{16,4},... | collective-permute-start | bytes 1769480 | tf_op jit(solution)/shard_map/ppermute | solution.py:204
  158.3 102.4 %collective-permute-start = (bf16[2,1,144,1024]{3,2,0,1:T(8,128)(2,1)S(1)}, bf16[2,1,144,1024]{3,2,0,1:T(8,128)(2,1)S(1)}, u32[]{:S(2)}, u32[]{:S(2)}) collective-permute-start(bf16[2,1,144,1024]{3,2,0,1:T(8,128)(2,1)S(1)} %bitcast.158), channel_id=1, source_target_pairs={{0,28},{2,30},{4,24},{6,26},{8,20},{10,22},{12,16},{14,18},{16,12}... | collective-permute-start | bytes 1769480 | tf_op jit(solution)/shard_map/ppermute | solution.py:204
  187.4 8.7 %copy-start.3 = (bf16[16,1,128,1024]{3,2,1,0:T(8,128)(2,1)S(1)}, bf16[16,1,128,1024]{3,2,1,0:T(8,128)(2,1)}, u32[]{:S(2)}) copy-start(bf16[16,1,128,1024]{3,2,1,0:T(8,128)(2,1)} %all-gather.4.cloned.1.call-done.q_ref) | copy-start | bytes 12582916
  196.0 10.1 %copy-start.4 = (bf16[64,1,128,128]{3,2,1,0:T(8,128)(2,1)S(1)}, bf16[64,1,128,128]{3,2,1,0:T(8,128)(2,1)}, u32[]{:S(2)}) copy-start(bf16[64,1,128,128]{3,2,1,0:T(8,128)(2,1)} %get-tuple-element.43.k_ref) | copy-start | bytes 6291460
  196.0 10.1 %copy-start.11 = (bf16[2,1,128,1024]{3,2,1,0:T(8,128)(2,1)S(1)}, bf16[2,1,128,1024]{3,2,1,0:T(8,128)(2,1)}, u32[]{:S(2)}) copy-start(bf16[2,1,128,1024]{3,2,1,0:T(8,128)(2,1)} %squeeze.137.q_ref) | copy-start | bytes 1572868
  196.0 79.7 %collective-permute-start.3 = (bf16[2,1,144,1024]{3,2,0,1:T(8,128)(2,1)S(1)}, bf16[2,1,144,1024]{3,2,0,1:T(8,128)(2,1)S(1)}, u32[]{:S(2)}, u32[]{:S(2)}) collective-permute-start(bf16[2,1,144,1024]{3,2,0,1:T(8,128)(2,1)S(1)} %bitcast.155), channel_id=1, source_target_pairs={{0,16},{2,18},{4,20},{6,22},{8,24},{10,26},{12,28},{14,30},{16,0},... | collective-permute-start | bytes 1769480 | tf_op jit(solution)/shard_map/ppermute | solution.py:204
  206.0 70.6 %collective-permute-start.1 = (bf16[2,1,144,1024]{3,2,0,1:T(8,128)(2,1)S(1)}, bf16[2,1,144,1024]{3,2,0,1:T(8,128)(2,1)S(1)}, u32[]{:S(2)}, u32[]{:S(2)}) collective-permute-start(bf16[2,1,144,1024]{3,2,0,1:T(8,128)(2,1)S(1)} %bitcast.156), channel_id=1, source_target_pairs={{0,24},{2,26},{4,28},{6,30},{8,16},{10,18},{12,20},{14,22},{16,8},... | collective-permute-start | bytes 1769480 | tf_op jit(solution)/shard_map/ppermute | solution.py:204
  206.1 42.6 %copy-start.10 = (bf16[64,1,128,128]{3,2,1,0:T(8,128)(2,1)S(1)}, bf16[64,1,128,128]{3,2,1,0:T(8,128)(2,1)}, u32[]{:S(2)}) copy-start(bf16[64,1,128,128]{3,2,1,0:T(8,128)(2,1)} %get-tuple-element.44.k_ref) | copy-start | bytes 6291460
  216.9 43.7 %copy-start.13 = (f32[2,1,144,1024]{3,2,1,0:T(8,128)}, f32[2,1,144,1024]{3,2,1,0:T(8,128)S(1)}, u32[]{:S(2)}) copy-start(f32[2,1,144,1024]{3,2,1,0:T(8,128)S(1)} %shard_map.81) | copy-start | bytes 3538948
  248.7 11.9 %copy-start.15 = (bf16[2,1,144,1024]{3,2,0,1:T(8,128)(2,1)}, bf16[2,1,144,1024]{3,2,0,1:T(8,128)(2,1)S(1)}, u32[]{:S(2)}) copy-start(bf16[2,1,144,1024]{3,2,0,1:T(8,128)(2,1)S(1)} %collective-permute-done.2) | copy-start | bytes 1769476
  260.6 80.6 %collective-permute-start.6 = (bf16[2,1,144,1024]{3,2,1,0:T(8,128)(2,1)}, bf16[2,1,144,1024]{3,2,1,0:T(8,128)(2,1)}, u32[]{:S(2)}, u32[]{:S(2)}) collective-permute-start(bf16[2,1,144,1024]{3,2,1,0:T(8,128)(2,1)} %shard_map.80), channel_id=1, source_target_pairs={{0,4},{2,6},{4,0},{6,2},{8,12},{10,14},{12,8},{14,10},{16,20},{18,... | collective-permute-start | bytes 1769480 | tf_op jit(solution)/shard_map/ppermute | solution.py:204
  260.7 9.3 %copy-start.17 = (bf16[2,1,144,1024]{3,2,0,1:T(8,128)(2,1)}, bf16[2,1,144,1024]{3,2,0,1:T(8,128)(2,1)S(1)}, u32[]{:S(2)}) copy-start(bf16[2,1,144,1024]{3,2,0,1:T(8,128)(2,1)S(1)} %collective-permute-done) | copy-start | bytes 1769476
  270.0 80.7 %collective-permute-start.4 = (bf16[2,1,144,1024]{3,2,0,1:T(8,128)(2,1)}, bf16[2,1,144,1024]{3,2,0,1:T(8,128)(2,1)}, u32[]{:S(2)}, u32[]{:S(2)}) collective-permute-start(bf16[2,1,144,1024]{3,2,0,1:T(8,128)(2,1)} %bitcast.41), channel_id=1, source_target_pairs={{0,12},{2,14},{4,8},{6,10},{8,4},{10,6},{12,0},{14,2},{16,28},{18,... | collective-permute-start | bytes 1769480 | tf_op jit(solution)/shard_map/ppermute | solution.py:204
  275.7 0.8 copy-start.19
  276.6 10.6 %copy-start.22 = (bf16[2,1,144,1024]{3,2,0,1:T(8,128)(2,1)}, bf16[2,1,144,1024]{3,2,0,1:T(8,128)(2,1)S(1)}, u32[]{:S(2)}) copy-start(bf16[2,1,144,1024]{3,2,0,1:T(8,128)(2,1)S(1)} %collective-permute-done.1) | copy-start | bytes 1769476
  287.2 64.3 %collective-permute-start.5 = (bf16[2,1,144,1024]{3,2,0,1:T(8,128)(2,1)}, bf16[2,1,144,1024]{3,2,0,1:T(8,128)(2,1)}, u32[]{:S(2)}, u32[]{:S(2)}) collective-permute-start(bf16[2,1,144,1024]{3,2,0,1:T(8,128)(2,1)} %bitcast.44), channel_id=1, source_target_pairs={{0,8},{2,10},{4,12},{6,14},{8,0},{10,2},{12,4},{14,6},{16,24},{18,... | collective-permute-start | bytes 1769480 | tf_op jit(solution)/shard_map/ppermute | solution.py:204
  296.1 2.2 copy-start
  298.3 1.6 copy-start.5
  299.9 1.1 copy-start.20
  301.0 40.1 %copy-start.18 = (bf16[2,1,144,1024]{3,2,0,1:T(8,128)(2,1)S(1)}, bf16[2,1,144,1024]{3,2,0,1:T(8,128)(2,1)}, u32[]{:S(2)}) copy-start(bf16[2,1,144,1024]{3,2,0,1:T(8,128)(2,1)} %copy-done.17) | copy-start | bytes 1769476
  301.0 40.2 %copy-start.23 = (bf16[2,1,144,1024]{3,2,0,1:T(8,128)(2,1)S(1)}, bf16[2,1,144,1024]{3,2,0,1:T(8,128)(2,1)}, u32[]{:S(2)}) copy-start(bf16[2,1,144,1024]{3,2,0,1:T(8,128)(2,1)} %copy-done.22) | copy-start | bytes 1769476
  305.9 48.9 %collective-permute-start.7 = (bf16[2,1,144,1024]{3,2,0,1:T(8,128)(2,1)S(1)}, bf16[2,1,144,1024]{3,2,0,1:T(8,128)(2,1)S(1)}, u32[]{:S(2)}, u32[]{:S(2)}) collective-permute-start(bf16[2,1,144,1024]{3,2,0,1:T(8,128)(2,1)S(1)} %bitcast.161), channel_id=1, source_target_pairs={{0,28},{2,30},{4,24},{6,26},{8,20},{10,22},{12,16},{14,18},{16,12}... | collective-permute-start | bytes 1769480 | tf_op jit(solution)/shard_map/ppermute | solution.py:204
  349.8 103.2 %collective-permute-start.10 = (bf16[2,1,144,1024]{3,2,0,1:T(8,128)(2,1)S(1)}, bf16[2,1,144,1024]{3,2,0,1:T(8,128)(2,1)S(1)}, u32[]{:S(2)}, u32[]{:S(2)}) collective-permute-start(bf16[2,1,144,1024]{3,2,0,1:T(8,128)(2,1)S(1)} %bitcast.152), channel_id=1, source_target_pairs={{0,16},{2,18},{4,20},{6,22},{8,24},{10,26},{12,28},{14,30},{16,0},... | collective-permute-start | bytes 1769480 | tf_op jit(solution)/shard_map/ppermute | solution.py:204
  354.9 22.8 %copy-start.1 = (bf16[16,1,128,1024]{3,2,1,0:T(8,128)(2,1)S(1)}, bf16[16,1,128,1024]{3,2,1,0:T(8,128)(2,1)}, u32[]{:S(2)}) copy-start(bf16[16,1,128,1024]{3,2,1,0:T(8,128)(2,1)} %all-gather.6.cloned.1.call-done.q_ref) | copy-start | bytes 12582916
  363.5 89.6 %collective-permute-start.11 = (bf16[2,1,144,1024]{3,2,0,1:T(8,128)(2,1)S(1)}, bf16[2,1,144,1024]{3,2,0,1:T(8,128)(2,1)S(1)}, u32[]{:S(2)}, u32[]{:S(2)}) collective-permute-start(bf16[2,1,144,1024]{3,2,0,1:T(8,128)(2,1)S(1)} %bitcast.153), channel_id=1, source_target_pairs={{0,12},{2,14},{4,8},{6,10},{8,4},{10,6},{12,0},{14,2},{16,28},{18,... | collective-permute-start | bytes 1769480 | tf_op jit(solution)/shard_map/ppermute | solution.py:204
  387.5 18.0 %collective-permute-start.8 = (bf16[2,1,144,1024]{3,2,0,1:T(8,128)(2,1)S(1)}, bf16[2,1,144,1024]{3,2,0,1:T(8,128)(2,1)S(1)}, u32[]{:S(2)}, u32[]{:S(2)}) collective-permute-start(bf16[2,1,144,1024]{3,2,0,1:T(8,128)(2,1)S(1)} %bitcast.154), channel_id=1, source_target_pairs={{0,24},{2,26},{4,28},{6,30},{8,16},{10,18},{12,20},{14,22},{16,8},... | collective-permute-start | bytes 1769480 | tf_op jit(solution)/shard_map/ppermute | solution.py:204
  391.2 11.4 %copy-start.16 = (bf16[2,1,144,1024]{3,2,0,1:T(8,128)(2,1)S(1)}, bf16[2,1,144,1024]{3,2,0,1:T(8,128)(2,1)}, u32[]{:S(2)}) copy-start(bf16[2,1,144,1024]{3,2,0,1:T(8,128)(2,1)} %copy-done.15) | copy-start | bytes 1769476
  391.2 11.4 %copy-start.21 = (bf16[2,1,144,1024]{3,2,0,1:T(8,128)(2,1)S(1)}, bf16[2,1,144,1024]{3,2,0,1:T(8,128)(2,1)}, u32[]{:S(2)}) copy-start(bf16[2,1,144,1024]{3,2,0,1:T(8,128)(2,1)} %copy-done.19) | copy-start | bytes 1769476
  402.4 39.1 %collective-permute-start.9 = (bf16[2,1,144,1024]{3,2,1,0:T(8,128)(2,1)S(1)}, bf16[2,1,144,1024]{3,2,1,0:T(8,128)(2,1)S(1)}, u32[]{:S(2)}, u32[]{:S(2)}) collective-permute-start(bf16[2,1,144,1024]{3,2,1,0:T(8,128)(2,1)S(1)} %shard_map.84), channel_id=1, source_target_pairs={{0,20},{2,22},{4,16},{6,18},{8,28},{10,30},{12,24},{14,26},{16,4},... | collective-permute-start | bytes 1769480 | tf_op jit(solution)/shard_map/ppermute | solution.py:204
  415.4 39.4 %collective-permute-start.12 = (bf16[2,1,144,1024]{3,2,0,1:T(8,128)(2,1)S(1)}, bf16[2,1,144,1024]{3,2,0,1:T(8,128)(2,1)S(1)}, u32[]{:S(2)}, u32[]{:S(2)}) collective-permute-start(bf16[2,1,144,1024]{3,2,0,1:T(8,128)(2,1)S(1)} %bitcast.157), channel_id=1, source_target_pairs={{0,8},{2,10},{4,12},{6,14},{8,0},{10,2},{12,4},{14,6},{16,24},{18,... | collective-permute-start | bytes 1769480 | tf_op jit(solution)/shard_map/ppermute | solution.py:204
  452.7 13.3 %copy-start.14 = (f32[2,1,144,1024]{3,2,1,0:T(8,128)S(1)}, f32[2,1,144,1024]{3,2,1,0:T(8,128)}, u32[]{:S(2)}) copy-start(f32[2,1,144,1024]{3,2,1,0:T(8,128)} %copy-done.13) | copy-start | bytes 3538948
  452.7 13.1 %collective-permute-start.13 = (bf16[2,1,144,1024]{3,2,0,1:T(8,128)(2,1)S(1)}, bf16[2,1,144,1024]{3,2,0,1:T(8,128)(2,1)S(1)}, u32[]{:S(2)}, u32[]{:S(2)}) collective-permute-start(bf16[2,1,144,1024]{3,2,0,1:T(8,128)(2,1)S(1)} %bitcast.159), channel_id=1, source_target_pairs={{0,4},{2,6},{4,0},{6,2},{8,12},{10,14},{12,8},{14,10},{16,20},{18,... | collective-permute-start | bytes 1769480 | tf_op jit(solution)/shard_map/ppermute | solution.py:204
Sparse Core Ops, SparseCore 0:
  40.3 73.9 all-gather.3
  116.4 134.5 all-gather.5

commit v4 on v3

--- a/solution.py
+++ b/solution.py
@@ -15,41 +15,55 @@
 SCALE = 1.4426950408889634 / math.sqrt(HD)
 STEP = 256
 EXTRA = 16
+BATCH = 4
 
 
 def attend_kernel(width, fresh, qsel, gsel, counts, ids, q_ref, k_ref, vt_ref, *rest):
     if fresh:
         kf_ref, vf_ref, *rest = rest
-    o_ref, acc = rest[-2:]
+    o_ref, acc, s_scr, w_scr = rest[-4:]
     i = pl.program_id(0)
     g = gsel[i]
     n = counts[g]
     heads = o_ref.shape[1]
     tiles = [(c, j) for c in range(heads) for j in range(ROWS // STEP)]
 
-    def fold(keys, vals_t, mask, second, carry):
-        out = []
-        for (c, j), (top, total) in zip(tiles, carry):
+    def fold(keys, vals_t, mask, alive, carry):
+        rows = len(alive) * 128
+        news, totals = [], []
+        for (c, j), (top, _) in zip(tiles, carry):
             cols = pl.ds(j * STEP, STEP)
-            s = jnp.dot(keys[c], q_ref[0, c, :, cols], preferred_element_type=jnp.float32)
-            if mask is not None:
-                s = jnp.where(mask, s, LOW)
-            here = jnp.max(s[:128], axis=0, keepdims=True)
-            if second is not None:
-                there = jnp.max(s[128:], axis=0, keepdims=True)
-                here = jnp.maximum(here, jnp.where(second, there, LOW))
-            new = jnp.maximum(top, here * SCALE)
-            w = jnp.exp2(s[:128] * SCALE - new)
-            if second is not None:
-                far = jnp.where(second, new, -LOW)
-                w = jnp.concatenate([w, jnp.exp2(s[128:] * SCALE - far)], axis=0)
-            fade = jnp.exp2(top - new)
-            total = total * fade + jnp.sum(w.reshape(w.shape[0] // 8, 8, STEP), axis=0)
-            acc[c, :, cols] = acc[c, :, cols] * fade + jnp.dot(
-                vals_t[c], w.astype(jnp.bfloat16), preferred_element_type=jnp.float32
+            for at in range(0, rows, 256):
+                end = min(rows, at + 256)
+                s = jnp.dot(
+                    keys[c][at:end], q_ref[0, c, :, cols], preferred_element_type=jnp.float32
+                )
+                s = s * SCALE
+                if mask is not None:
+                    s = jnp.where(mask, s, LOW)
+                s_scr[c, at:end, cols] = s
+                for k in range(at, end, 128):
+                    here = jnp.max(s[k - at : k - at + 128], axis=0, keepdims=True)
+                    if alive[k // 128] is not None:
+                        here = jnp.where(alive[k // 128], here, LOW)
+                    top = jnp.maximum(top, here)
+            news.append(top)
+        for (c, j), new, (top, total) in zip(tiles, news, carry):
+            cols = pl.ds(j * STEP, STEP)
+            total = total * jnp.exp2(top - new)
+            for k, live in enumerate(alive):
+                at = pl.ds(k * 128, 128)
+                far = new if live is None else jnp.where(live, new, -LOW)
+                w = jnp.exp2(s_scr[c, at, cols] - far)
+                total = total + jnp.sum(w.reshape(16, 8, STEP), axis=0)
+                w_scr[c, at, cols] = w.astype(jnp.bfloat16)
+            totals.append(total)
+        for (c, j), new, (top, _) in zip(tiles, news, carry):
+            cols = pl.ds(j * STEP, STEP)
+            acc[c, :, cols] = acc[c, :, cols] * jnp.exp2(top - new) + jnp.dot(
+                vals_t[c], w_scr[c, :rows, cols], preferred_element_type=jnp.float32
             )
-            out.append((new, total))
-        return tuple(out)
+        return tuple(zip(news, totals))
 
     acc[...] = jnp.zeros_like(acc)
     carry = tuple(
@@ -62,21 +76,21 @@
             [kf_ref[i, c] for c in range(heads)],
             [vf_ref[i, c] for c in range(heads)],
             row <= col % 128,
-            None,
+            [None],
             carry,
         )
 
-    def pair(p, carry):
-        one, two = ids[g * width + 2 * p], ids[g * width + 2 * p + 1]
+    def batch(p, carry):
+        which = [ids[g * width + BATCH * p + k] for k in range(BATCH)]
         return fold(
-            [jnp.concatenate([k_ref[one, c], k_ref[two, c]], axis=0) for c in range(heads)],
-            [jnp.concatenate([vt_ref[one, c], vt_ref[two, c]], axis=1) for c in range(heads)],
+            [jnp.concatenate([k_ref[i, c] for i in which], axis=0) for c in range(heads)],
+            [jnp.concatenate([vt_ref[i, c] for i in which], axis=1) for c in range(heads)],
             None,
-            2 * p + 1 < n,
+            [None] + [BATCH * p + k < n for k in range(1, BATCH)],
             carry,
         )
 
-    carry = lax.fori_loop(0, (n + 1) // 2, pair, carry)
+    carry = lax.fori_loop(0, (n + BATCH - 1) // BATCH, batch, carry)
     for (c, j), (top, total) in zip(tiles, carry):
         cols = pl.ds(j * STEP, STEP)
         total = jnp.sum(total, axis=0, keepdims=True)
@@ -112,6 +126,8 @@
             out_specs=pl.BlockSpec((1, heads, HD + EXTRA, ROWS), lambda i, *_: (i, 0, 0, 0)),
             scratch_shapes=[
                 pltpu.VMEM((heads, HD, ROWS), jnp.float32),
+                pltpu.VMEM((heads, BATCH * 128, ROWS), jnp.float32),
+                pltpu.VMEM((heads, BATCH * 128, ROWS), jnp.bfloat16),
             ],
         ),
         out_shape=jax.ShapeDtypeStruct(
@@ -153,7 +169,8 @@
     mine = (code >= 0) & (code // (span * pool) == unit)
     counts = jnp.sum(mine.astype(jnp.int32), axis=1)
     rank = jnp.cumsum(mine.astype(jnp.int32), axis=1) - 1
-    width = min(span * max(2, 2 * slots // groups), slots) + 2
+    width = min(span * max(2, 2 * slots // groups), slots)
+    width = -(-width // BATCH) * BATCH
     hit = mine[:, None, :] & (rank[:, None, :] == jnp.arange(width)[None, :, None])
     ids = jnp.sum(jnp.where(hit, (code % (span * pool))[:, None, :], 0), axis=-1)
 

time: 511 us -> 463 us (0.906); the launches traced: 503 us -> 461 us
  Pallas kernels: 152 us -> 93.5 us
  waiting for transfers between devices: 50.3 us -> 99.5 us
  starting transfers between devices: 128 us -> 95.4 us
    pallas_call x16, Pallas kernels: 152 us -> 93.5 us  [attend(): pl.pallas_call(functools.partial(attend_kernel, width, fresh is not None)...]
    ppermute x14, waiting for transfers between devices: 50.3 us -> 99.5 us  [local(): arrived[c].append(lax.ppermute(part[k * span:(k + 1) * span], 'dp', to))]
    ppermute x14, starting transfers between devices: 121 us -> 88.1 us  [local(): arrived[c].append(lax.ppermute(part[k * span:(k + 1) * span], 'dp', to))]
  transfers between devices with their start and end apart: 17 -> 17, of which waited for: 6 -> 7; matrix products, arithmetic and copies ran while one was open for 11% -> 12% of each run, Pallas kernels for 30% -> 20%
where the time goes in v4:
time: 463 us; the launch traced here: 461 us
  waiting for transfers between devices  99.5 us (21%)
  starting transfers between devices  95.4 us (21%)
  Pallas kernels  93.5 us (20%)
  local copies, waits for them, and re-layouts  80.8 us (17%)
  blocking collectives  68.3 us (15%)
  between operations  14.8 us (3%)
  other arithmetic  9.17 us (2%)
    ppermute x14, waiting for transfers between devices, local(): arrived[c].append(lax.ppermute(part[k * span:(k + 1) * span], 'dp', to))  99.5 us
    pallas_call x16, Pallas kernels, attend(): pl.pallas_call(functools.partial(attend_kernel, width, fresh is not None)...  93.5 us
    ppermute x14, starting transfers between devices, local(): arrived[c].append(lax.ppermute(part[k * span:(k + 1) * span], 'dp', to))  88.1 us
    unnamed x72, local copies, waits for them, and re-layouts  52.8 us
    all_to_all x4, blocking collectives, exchange(): lax.all_to_all(x, axis, split_axis=split, concat_axis=concat, tiled=True,...  46.4 us
    all_gather x1, blocking collectives, local(): code = lax.all_gather(code, 'dp', axis=0, tiled=True)  21.9 us
  transfers between devices with their start and end apart: 17, of which 7 were waited for; matrix products, arithmetic and copies ran while one was open for 12% of the time, Pallas kernels for 20%

profile of v4, /device:TPU:0, one launch (start us, length us, event | category | flops | bytes accessed | tf_op | source)
XLA Modules:
  0.0 461.5 jit_solution(4417001436327135007)
XLA Ops:
  6.5 1.9 reshape.452
  10.4 20.4 %all_to_all.45 = bf16[64,2,5120]{2,0,1:T(8,128)(2,1)S(1)} all-to-all(bf16[64,2,5120]{2,0,1:T(8,128)(2,1)S(1)} %copy.214), channel_id=1, replica_groups=mesh['dp'=16,'tensor'=2] {'tensor'}, dimensions={1} | all-to-all | bytes 2621440 | tf_op jit(solution)/shard_map/all_to_all | solution.py:144
  31.9 4.8 %all_to_all.46 = bf16[2,128,2560]{2,1,0:T(8,128)(2,1)S(1)} all-to-all(bf16[2,128,2560]{2,1,0:T(8,128)(2,1)S(1)} %copy.215), channel_id=1, replica_groups={{0,2},{4,6},{8,10},{12,14},{16,18},{20,22},{24,26},{28,30},{1,3},{5,7},..., dimensions={0} | all-to-all | bytes 2621440 | tf_op jit(solution)/shard_map/all_to_all | solution.py:144
  41.6 21.2 %copy.218 = bf16[32,128,2,512]{1,3,2,0:T(8,128)(2,1)} copy(bf16[32,128,2,512]{3,2,1,0:T(2,128)(2,1)} %param.10) | data formatting | bytes 16777216 | tf_op args[3]
  62.8 7.7 %copy.219 = bf16[2,32,2,128,256]{3,4,2,1,0:T(8,128)(2,1)} copy(bf16[2,32,2,128,256]{3,4,0,2,1:T(8,128)(2,1)} %bitcast.162) | data formatting | bytes 16777216 | tf_op jit(solution)/shard_map/transpose | solution.py:193
  70.6 7.2 %all-to-all-start.2 = ((bf16[2,32,2,128,256]{3,4,2,1,0:T(8,128)(2,1)}), bf16[2,32,2,128,256]{3,4,2,1,0:T(8,128)(2,1)}, u32[]{:S(2)}, u32[]{:S(2)}) async-start(bf16[2,32,2,128,256]{3,4,2,1,0:T(8,128)(2,1)} %copy.219), calls=%async_computation.2 | async-start | bytes 16777216 | tf_op jit(solution)/shard_map/all_to_all | solution.py:144
  78.5 21.9 %all-gather = s32[16,1,64]{2,1,0:T(1,128)S(1)} all-gather(s32[1,1,64]{2,1,0:T(1,128)S(1)} %fusion.20), channel_id=1, replica_groups=mesh['dp'=16,'tensor'=2] {'dp'}, dimensions={0}, use_global_device_ids=true | all-gather | bytes 4352 | tf_op jit(solution)/shard_map/all_gather | solution.py:168
  101.1 5.4 %fusion.38 = (bf16[64,1,128,2,1,128]{2,5,3,1,0,4:T(8,128)(2,1)S(1)}, bf16[64,1,128,2,1,128]{2,5,3,1,0,4:T(8,128)(2,1)}) fusion(bf16[64,2,128,2,1,128]{2,5,3,1,0,4:T(8,128)(2,1)} %bitcast.11), kind=kLoop, calls=%fused_computation.109 | loop fusion | bytes 16777216 | tf_op jit(solution)/shard_map/slice | solution.py:198
  106.5 2.2 copy.280
  108.8 6.4 %copy.270 = bf16[64,1,128,2,1,128]{5,2,0,3,4,1:T(8,128)(2,1)} copy(bf16[64,1,128,2,1,128]{2,5,3,1,0,4:T(8,128)(2,1)} %get-tuple-element.14) | data formatting | bytes 8388608
  115.3 5.7 %slice_bitcast_fusion.2 = (bf16[64,1,128,128]{3,2,1,0:T(8,128)(2,1)}, bf16[64,1,128,128]{3,2,1,0:T(8,128)(2,1)S(1)}, bf16[64,1,128,128]{3,2,1,0:T(8,128)(2,1)}, bf16[64,1,128,128]{3,2,1,0:T(8,128)(2,1)}) fusion(bf16[2,64,1,128,128]{4,3,1,2,0:T(8,128)(2,1)} %bitcast.163, bf16[2,64,1,128,128]{4,3,1,2,0:T(8,128)(2,1)} %bitcast.164), kind=kLoop, calls=%fused_computation.3 | loop fusion | bytes 16777216 | tf_op jit(solution)/shard_map/squeeze | solution.py:207
  121.5 1.7 copy-done.6
  123.2 1.7 copy-done.8
  126.0 5.9 %shard_map.73.rest_0_ = f32[2,1,144,1024]{3,2,1,0:T(8,128)S(1)} custom-call(s32[2]{0:T(128)S(1)} %iota.29.qsel, s32[2]{0:T(128)S(1)} %iota_add_fusion.7.gsel, s32[16]{0:T(128)S(1)} %convert_reduce_fusion.14.counts, s32[256]{0:T(256)S(1)} %reshape.451.ids, bf16[2,1,128,1024]{3,2,1,0:T(8,128)(2,1)S(1)} %copy-done.12, bf16[64,1,128,128]{3,2,1,0:T(8,128)(2,1)S(1)} %copy-done.8, ...), custom_call_target="tpu_custom_call" | custom-call | flops 1073741824 | bytes 1048576 | tf_op jit(solution)/shard_map/pallas_call | solution.py:118
  132.0 2.2 copy-done
  135.8 1.6 copy-done.9
  137.4 5.4 %shard_map.76 = bf16[2,1,144,1024]{3,2,1,0:T(8,128)(2,1)S(1)} custom-call(s32[2]{0:T(128)S(1)} %iota_add_fusion.4.qsel.gsel, s32[2]{0:T(128)S(1)} %iota_add_fusion.4.qsel.gsel, s32[16]{0:T(128)S(1)} %convert_reduce_fusion.14.counts, s32[256]{0:T(256)S(1)} %reshape.451.ids, bf16[16,1,128,1024]{3,2,1,0:T(8,128)(2,1)S(1)} %copy-done, ...), custom_call_target="tpu_custom_call" | custom-call | flops 1073741824 | bytes 1048576 | tf_op jit(solution)/shard_map/pallas_call | solution.py:118
  142.9 5.4 %shard_map.74 = bf16[2,1,144,1024]{3,2,1,0:T(8,128)(2,1)S(1)} custom-call(s32[2]{0:T(128)S(1)} %iota_add_fusion.6.qsel.gsel, s32[2]{0:T(128)S(1)} %iota_add_fusion.6.qsel.gsel, s32[16]{0:T(128)S(1)} %convert_reduce_fusion.14.counts, s32[256]{0:T(256)S(1)} %reshape.451.ids, bf16[16,1,128,1024]{3,2,1,0:T(8,128)(2,1)S(1)} %copy-done, ...), custom_call_target="tpu_custom_call" | custom-call | flops 1073741824 | bytes 1048576 | tf_op jit(solution)/shard_map/pallas_call | solution.py:118
  148.2 3.8 collective-permute-start
  152.0 5.4 %shard_map.77 = bf16[2,1,144,1024]{3,2,1,0:T(8,128)(2,1)S(1)} custom-call(s32[2]{0:T(128)S(1)} %iota_add_fusion.3.qsel.gsel, s32[2]{0:T(128)S(1)} %iota_add_fusion.3.qsel.gsel, s32[16]{0:T(128)S(1)} %convert_reduce_fusion.14.counts, s32[256]{0:T(256)S(1)} %reshape.451.ids, bf16[16,1,128,1024]{3,2,1,0:T(8,128)(2,1)S(1)} %copy-done, ...), custom_call_target="tpu_custom_call" | custom-call | flops 1073741824 | bytes 1048576 | tf_op jit(solution)/shard_map/pallas_call | solution.py:118
  157.5 6.3 %shard_map.75 = bf16[2,1,144,1024]{3,2,1,0:T(8,128)(2,1)S(1)} custom-call(s32[2]{0:T(128)S(1)} %iota_add_fusion.5.qsel.gsel, s32[2]{0:T(128)S(1)} %iota_add_fusion.5.qsel.gsel, s32[16]{0:T(128)S(1)} %convert_reduce_fusion.14.counts, s32[256]{0:T(256)S(1)} %reshape.451.ids, bf16[16,1,128,1024]{3,2,1,0:T(8,128)(2,1)S(1)} %copy-done.1, ...), custom_call_target="tpu_custom_call" | custom-call | flops 1073741824 | bytes 1048576 | tf_op jit(solution)/shard_map/pallas_call | solution.py:118
  165.1 5.9 %shard_map.81 = f32[2,1,144,1024]{3,2,1,0:T(8,128)S(1)} custom-call(s32[2]{0:T(128)S(1)} %iota.39.qsel, s32[2]{0:T(128)S(1)} %iota_add_fusion.7.gsel, s32[16]{0:T(128)S(1)} %convert_reduce_fusion.14.counts, s32[256]{0:T(256)S(1)} %reshape.451.ids, bf16[2,1,128,1024]{3,2,1,0:T(8,128)(2,1)S(1)} %copy-done.11, bf16[64,1,128,128]{3,2,1,0:T(8,128)(2,1)S(1)} %copy-done.4, ...), custom_call_target="tpu_custom_call" | custom-call | flops 1073741824 | bytes 1048576 | tf_op jit(solution)/shard_map/pallas_call | solution.py:118
  171.0 53.7 %collective-permute-done.2 = bf16[2,1,144,1024]{3,2,0,1:T(8,128)(2,1)S(1)} collective-permute-done((bf16[2,1,144,1024]{3,2,0,1:T(8,128)(2,1)S(1)}, bf16[2,1,144,1024]{3,2,0,1:T(8,128)(2,1)S(1)}, u32[]{:S(2)}, u32[]{:S(2)}) %collective-permute-start.2) | collective-permute-done | bytes 589856 | tf_op jit(solution)/shard_map/ppermute | solution.py:221
  224.8 6.1 %shard_map.80 = bf16[2,1,144,1024]{3,2,1,0:T(8,128)(2,1)} custom-call(s32[2]{0:T(128)S(1)} %iota_add_fusion.qsel.gsel, s32[2]{0:T(128)S(1)} %iota_add_fusion.qsel.gsel, s32[16]{0:T(128)S(1)} %convert_reduce_fusion.14.counts, s32[256]{0:T(256)S(1)} %reshape.451.ids, bf16[16,1,128,1024]{3,2,1,0:T(8,128)(2,1)S(1)} %copy-done.1, ...), custom_call_target="tpu_custom_call" | custom-call | flops 1073741824 | bytes 1048576 | tf_op jit(solution)/shard_map/pallas_call | solution.py:118
  230.9 6.1 %shard_map.78 = bf16[2,1,144,1024]{3,2,1,0:T(8,128)(2,1)} custom-call(s32[2]{0:T(128)S(1)} %iota_add_fusion.2.qsel.gsel, s32[2]{0:T(128)S(1)} %iota_add_fusion.2.qsel.gsel, s32[16]{0:T(128)S(1)} %convert_reduce_fusion.14.counts, s32[256]{0:T(256)S(1)} %reshape.451.ids, bf16[16,1,128,1024]{3,2,1,0:T(8,128)(2,1)S(1)} %copy-done.1, ...), custom_call_target="tpu_custom_call" | custom-call | flops 1073741824 | bytes 1048576 | tf_op jit(solution)/shard_map/pallas_call | solution.py:118
  237.0 23.7 %collective-permute-start.4 = (bf16[2,1,144,1024]{3,2,0,1:T(8,128)(2,1)}, bf16[2,1,144,1024]{3,2,0,1:T(8,128)(2,1)}, u32[]{:S(2)}, u32[]{:S(2)}) collective-permute-start(bf16[2,1,144,1024]{3,2,0,1:T(8,128)(2,1)} %bitcast.41), channel_id=1, source_target_pairs={{0,12},{2,14},{4,8},{6,10},{8,4},{10,6},{12,0},{14,2},{16,28},{18,... | collective-permute-start | bytes 1769480 | tf_op jit(solution)/shard_map/ppermute | solution.py:221
  260.8 5.4 %collective-permute-done.3 = bf16[2,1,144,1024]{3,2,0,1:T(8,128)(2,1)S(1)} collective-permute-done((bf16[2,1,144,1024]{3,2,0,1:T(8,128)(2,1)S(1)}, bf16[2,1,144,1024]{3,2,0,1:T(8,128)(2,1)S(1)}, u32[]{:S(2)}, u32[]{:S(2)}) %collective-permute-start.3) | collective-permute-done | bytes 589856 | tf_op jit(solution)/shard_map/ppermute | solution.py:221
  267.0 7.0 %shard_map.79 = bf16[2,1,144,1024]{3,2,1,0:T(8,128)(2,1)} custom-call(s32[2]{0:T(128)S(1)} %iota_add_fusion.1.qsel.gsel, s32[2]{0:T(128)S(1)} %iota_add_fusion.1.qsel.gsel, s32[16]{0:T(128)S(1)} %convert_reduce_fusion.14.counts, s32[256]{0:T(256)S(1)} %reshape.451.ids, bf16[16,1,128,1024]{3,2,1,0:T(8,128)(2,1)S(1)} %copy-done.1, ...), custom_call_target="tpu_custom_call" | custom-call | flops 1073741824 | bytes 1048576 | tf_op jit(solution)/shard_map/pallas_call | solution.py:118
  274.0 11.9 %collective-permute-start.5 = (bf16[2,1,144,1024]{3,2,0,1:T(8,128)(2,1)}, bf16[2,1,144,1024]{3,2,0,1:T(8,128)(2,1)}, u32[]{:S(2)}, u32[]{:S(2)}) collective-permute-start(bf16[2,1,144,1024]{3,2,0,1:T(8,128)(2,1)} %bitcast.44), channel_id=1, source_target_pairs={{0,8},{2,10},{4,12},{6,14},{8,0},{10,2},{12,4},{14,6},{16,24},{18,... | collective-permute-start | bytes 1769480 | tf_op jit(solution)/shard_map/ppermute | solution.py:221
  285.9 2.2 copy-done.2
  290.8 5.4 %shard_map.82 = bf16[2,1,144,1024]{3,2,1,0:T(8,128)(2,1)S(1)} custom-call(s32[2]{0:T(128)S(1)} %iota_add_fusion.6.qsel.gsel, s32[2]{0:T(128)S(1)} %iota_add_fusion.6.qsel.gsel, s32[16]{0:T(128)S(1)} %convert_reduce_fusion.14.counts, s32[256]{0:T(256)S(1)} %reshape.451.ids, bf16[16,1,128,1024]{3,2,1,0:T(8,128)(2,1)S(1)} %copy-done.2, ...), custom_call_target="tpu_custom_call" | custom-call | flops 1073741824 | bytes 1048576 | tf_op jit(solution)/shard_map/pallas_call | solution.py:118
  296.2 2.9 collective-permute-start.7
  299.1 5.6 %shard_map.85 = bf16[2,1,144,1024]{3,2,1,0:T(8,128)(2,1)S(1)} custom-call(s32[2]{0:T(128)S(1)} %iota_add_fusion.3.qsel.gsel, s32[2]{0:T(128)S(1)} %iota_add_fusion.3.qsel.gsel, s32[16]{0:T(128)S(1)} %convert_reduce_fusion.14.counts, s32[256]{0:T(256)S(1)} %reshape.451.ids, bf16[16,1,128,1024]{3,2,1,0:T(8,128)(2,1)S(1)} %copy-done.2, ...), custom_call_target="tpu_custom_call" | custom-call | flops 1073741824 | bytes 1048576 | tf_op jit(solution)/shard_map/pallas_call | solution.py:118
  307.3 8.0 %collective-permute-done.7 = bf16[2,1,144,1024]{3,2,0,1:T(8,128)(2,1)S(1)} collective-permute-done((bf16[2,1,144,1024]{3,2,0,1:T(8,128)(2,1)S(1)}, bf16[2,1,144,1024]{3,2,0,1:T(8,128)(2,1)S(1)}, u32[]{:S(2)}, u32[]{:S(2)}) %collective-permute-start.7) | collective-permute-done | bytes 589856 | tf_op jit(solution)/shard_map/ppermute | solution.py:221
  315.3 5.4 %shard_map.86 = bf16[2,1,144,1024]{3,2,1,0:T(8,128)(2,1)S(1)} custom-call(s32[2]{0:T(128)S(1)} %iota_add_fusion.2.qsel.gsel, s32[2]{0:T(128)S(1)} %iota_add_fusion.2.qsel.gsel, s32[16]{0:T(128)S(1)} %convert_reduce_fusion.14.counts, s32[256]{0:T(256)S(1)} %reshape.451.ids, bf16[16,1,128,1024]{3,2,1,0:T(8,128)(2,1)S(1)} %copy-done.2, ...), custom_call_target="tpu_custom_call" | custom-call | flops 1073741824 | bytes 1048576 | tf_op jit(solution)/shard_map/pallas_call | solution.py:118
  320.7 27.6 %collective-permute-start.11 = (bf16[2,1,144,1024]{3,2,0,1:T(8,128)(2,1)S(1)}, bf16[2,1,144,1024]{3,2,0,1:T(8,128)(2,1)S(1)}, u32[]{:S(2)}, u32[]{:S(2)}) collective-permute-start(bf16[2,1,144,1024]{3,2,0,1:T(8,128)(2,1)S(1)} %bitcast.157), channel_id=1, source_target_pairs={{0,12},{2,14},{4,8},{6,10},{8,4},{10,6},{12,0},{14,2},{16,28},{18,... | collective-permute-start | bytes 1769480 | tf_op jit(solution)/shard_map/ppermute | solution.py:221
  348.3 6.3 %shard_map.83 = bf16[2,1,144,1024]{3,2,1,0:T(8,128)(2,1)S(1)} custom-call(s32[2]{0:T(128)S(1)} %iota_add_fusion.5.qsel.gsel, s32[2]{0:T(128)S(1)} %iota_add_fusion.5.qsel.gsel, s32[16]{0:T(128)S(1)} %convert_reduce_fusion.14.counts, s32[256]{0:T(256)S(1)} %reshape.451.ids, bf16[16,1,128,1024]{3,2,1,0:T(8,128)(2,1)S(1)} %copy-done.3, ...), custom_call_target="tpu_custom_call" | custom-call | flops 1073741824 | bytes 1048576 | tf_op jit(solution)/shard_map/pallas_call | solution.py:118
  354.8 5.4 %shard_map.84 = bf16[2,1,144,1024]{3,2,1,0:T(8,128)(2,1)S(1)} custom-call(s32[2]{0:T(128)S(1)} %iota_add_fusion.4.qsel.gsel, s32[2]{0:T(128)S(1)} %iota_add_fusion.4.qsel.gsel, s32[16]{0:T(128)S(1)} %convert_reduce_fusion.14.counts, s32[256]{0:T(256)S(1)} %reshape.451.ids, bf16[16,1,128,1024]{3,2,1,0:T(8,128)(2,1)S(1)} %copy-done.3, ...), custom_call_target="tpu_custom_call" | custom-call | flops 1073741824 | bytes 1048576 | tf_op jit(solution)/shard_map/pallas_call | solution.py:118
  360.4 2.3 fusion.15
  362.8 12.0 %collective-permute-done.8 = bf16[2,1,144,1024]{3,2,0,1:T(8,128)(2,1)S(1)} collective-permute-done((bf16[2,1,144,1024]{3,2,0,1:T(8,128)(2,1)S(1)}, bf16[2,1,144,1024]{3,2,0,1:T(8,128)(2,1)S(1)}, u32[]{:S(2)}, u32[]{:S(2)}) %collective-permute-start.8) | collective-permute-done | bytes 589856 | tf_op jit(solution)/shard_map/ppermute | solution.py:221
  374.8 6.4 %shard_map.87 = bf16[2,1,144,1024]{3,2,1,0:T(8,128)(2,1)S(1)} custom-call(s32[2]{0:T(128)S(1)} %iota_add_fusion.1.qsel.gsel, s32[2]{0:T(128)S(1)} %iota_add_fusion.1.qsel.gsel, s32[16]{0:T(128)S(1)} %convert_reduce_fusion.14.counts, s32[256]{0:T(256)S(1)} %reshape.451.ids, bf16[16,1,128,1024]{3,2,1,0:T(8,128)(2,1)S(1)} %copy-done.3, ...), custom_call_target="tpu_custom_call" | custom-call | flops 1073741824 | bytes 1048576 | tf_op jit(solution)/shard_map/pallas_call | solution.py:118
  381.1 16.5 %collective-permute-start.12 = (bf16[2,1,144,1024]{3,2,0,1:T(8,128)(2,1)S(1)}, bf16[2,1,144,1024]{3,2,0,1:T(8,128)(2,1)S(1)}, u32[]{:S(2)}, u32[]{:S(2)}) collective-permute-start(bf16[2,1,144,1024]{3,2,0,1:T(8,128)(2,1)S(1)} %bitcast.159), channel_id=1, source_target_pairs={{0,8},{2,10},{4,12},{6,14},{8,0},{10,2},{12,4},{14,6},{16,24},{18,... | collective-permute-start | bytes 1769480 | tf_op jit(solution)/shard_map/ppermute | solution.py:221
  397.7 8.1 %collective-permute-done.9.rest_0_ = bf16[2,1,144,1024]{3,2,1,0:T(8,128)(2,1)S(1)} collective-permute-done((bf16[2,1,144,1024]{3,2,1,0:T(8,128)(2,1)S(1)}, bf16[2,1,144,1024]{3,2,1,0:T(8,128)(2,1)S(1)}, u32[]{:S(2)}, u32[]{:S(2)}) %collective-permute-start.9) | collective-permute-done | bytes 589856 | tf_op jit(solution)/shard_map/ppermute | solution.py:221
  405.7 5.4 %shard_map.88 = bf16[2,1,144,1024]{3,2,1,0:T(8,128)(2,1)S(1)} custom-call(s32[2]{0:T(128)S(1)} %iota_add_fusion.qsel.gsel, s32[2]{0:T(128)S(1)} %iota_add_fusion.qsel.gsel, s32[16]{0:T(128)S(1)} %convert_reduce_fusion.14.counts, s32[256]{0:T(256)S(1)} %reshape.451.ids, bf16[16,1,128,1024]{3,2,1,0:T(8,128)(2,1)S(1)} %copy-done.3, ...), custom_call_target="tpu_custom_call" | custom-call | flops 1073741824 | bytes 1048576 | tf_op jit(solution)/shard_map/pallas_call | solution.py:118
  411.6 3.7 collective-permute-done.12
  415.4 8.6 %collective-permute-done.13 = bf16[2,1,144,1024]{3,2,0,1:T(8,128)(2,1)S(1)} collective-permute-done((bf16[2,1,144,1024]{3,2,0,1:T(8,128)(2,1)S(1)}, bf16[2,1,144,1024]{3,2,0,1:T(8,128)(2,1)S(1)}, u32[]{:S(2)}, u32[]{:S(2)}) %collective-permute-start.13) | collective-permute-done | bytes 589856 | tf_op jit(solution)/shard_map/ppermute | solution.py:221
  425.4 4.6 all_to_all.47
  433.3 16.6 %all_to_all.48 = bf16[2,2,131072]{2,1,0:T(2,128)(2,1)S(1)} all-to-all(bf16[2,2,131072]{2,1,0:T(2,128)(2,1)S(1)} %reshape.466), channel_id=1, replica_groups=mesh['dp'=16,'tensor'=2] {'tensor'}, dimensions={0} | all-to-all | bytes 2097152 | tf_op jit(solution)/shard_map/all_to_all | solution.py:144
  (147 shorter events, 29.4 us)
Async XLA Ops:
  6.5 1.9 copy-start.25
  6.5 2.0 copy-start.26
  6.5 125.4 %all-gather.4.cloned.1.call-start = ((), (), s32[]{:S(2)}) async-start(), calls=%async_computation.5 | async-start | bytes 4718592 | tf_op jit(solution)/shard_map/all_gather | solution.py:186
  36.7 1.2 copy-start.24
  40.2 245.7 %all-gather.6.cloned.1.call-start = ((), (), s32[]{:S(2)}) async-start(), calls=%async_computation.6 | async-start | bytes 4718592 | tf_op jit(solution)/shard_map/all_gather | solution.py:186
  70.6 7.9 %copy-start.27 = (s32[1,64]{1,0:T(1,128)S(1)}, s32[1,64]{1,0:T(1,128)}, u32[]{:S(2)}) copy-start(s32[1,64]{1,0:T(1,128)} %param.12) | copy-start | bytes 772
  70.6 7.9 %copy-start.28 = (s32[1,64,1]{1,2,0:T(1,128)S(1)}, s32[1,64,1]{1,2,0:T(1,128)}, u32[]{:S(2)}) copy-start(s32[1,64,1]{1,2,0:T(1,128)} %param.11) | copy-start | bytes 772
  70.6 30.5 %all-to-all-start.2 = ((bf16[2,32,2,128,256]{3,4,2,1,0:T(8,128)(2,1)}), bf16[2,32,2,128,256]{3,4,2,1,0:T(8,128)(2,1)}, u32[]{:S(2)}, u32[]{:S(2)}) async-start(bf16[2,32,2,128,256]{3,4,2,1,0:T(8,128)(2,1)} %copy.219), calls=%async_computation.2 | async-start | bytes 16777216 | tf_op jit(solution)/shard_map/all_to_all | solution.py:144
  115.3 5.7 %slice-start = ((bf16[2,128,2560]{2,1,0:T(8,128)(2,1)}), bf16[2,128,512]{2,1,0:T(8,128)(2,1)S(1)}, s32[]{:S(2)}) async-start(bf16[2,128,2560]{2,1,0:T(8,128)(2,1)} %copy-done.24), calls=%async_computation.7 | async-start | bytes 524288 | tf_op jit(solution)/shard_map/slice | solution.py:189
  121.4 1.8 copy-start.6
  123.2 1.7 copy-start.8
  124.9 1.0 copy-start.12
  131.9 2.2 copy-start
  134.1 1.6 copy-start.7
  135.8 1.6 copy-start.9
  142.7 82.0 %collective-permute-start.2 = (bf16[2,1,144,1024]{3,2,0,1:T(8,128)(2,1)S(1)}, bf16[2,1,144,1024]{3,2,0,1:T(8,128)(2,1)S(1)}, u32[]{:S(2)}, u32[]{:S(2)}) collective-permute-start(bf16[2,1,144,1024]{3,2,0,1:T(8,128)(2,1)S(1)} %bitcast.155), channel_id=1, source_target_pairs={{0,20},{2,22},{4,16},{6,18},{8,28},{10,30},{12,24},{14,26},{16,4},... | collective-permute-start | bytes 1769480 | tf_op jit(solution)/shard_map/ppermute | solution.py:221
  148.2 82.7 %collective-permute-start = (bf16[2,1,144,1024]{3,2,0,1:T(8,128)(2,1)S(1)}, bf16[2,1,144,1024]{3,2,0,1:T(8,128)(2,1)S(1)}, u32[]{:S(2)}, u32[]{:S(2)}) collective-permute-start(bf16[2,1,144,1024]{3,2,0,1:T(8,128)(2,1)S(1)} %bitcast.154), channel_id=1, source_target_pairs={{0,28},{2,30},{4,24},{6,26},{8,20},{10,22},{12,16},{14,18},{16,12}... | collective-permute-start | bytes 1769480 | tf_op jit(solution)/shard_map/ppermute | solution.py:221
  152.0 5.5 %copy-start.1 = (bf16[16,1,128,1024]{3,2,1,0:T(8,128)(2,1)S(1)}, bf16[16,1,128,1024]{3,2,1,0:T(8,128)(2,1)}, u32[]{:S(2)}) copy-start(bf16[16,1,128,1024]{3,2,1,0:T(8,128)(2,1)} %all-gather.4.cloned.1.call-done.q_ref) | copy-start | bytes 12582916
  157.4 7.7 %copy-start.4 = (bf16[64,1,128,128]{3,2,1,0:T(8,128)(2,1)S(1)}, bf16[64,1,128,128]{3,2,1,0:T(8,128)(2,1)}, u32[]{:S(2)}) copy-start(bf16[64,1,128,128]{3,2,1,0:T(8,128)(2,1)} %get-tuple-element.43.k_ref) | copy-start | bytes 6291460
  157.4 7.6 %copy-start.11 = (bf16[2,1,128,1024]{3,2,1,0:T(8,128)(2,1)S(1)}, bf16[2,1,128,1024]{3,2,1,0:T(8,128)(2,1)}, u32[]{:S(2)}) copy-start(bf16[2,1,128,1024]{3,2,1,0:T(8,128)(2,1)} %squeeze.137.q_ref) | copy-start | bytes 1572868
  157.4 108.7 %collective-permute-start.3 = (bf16[2,1,144,1024]{3,2,0,1:T(8,128)(2,1)S(1)}, bf16[2,1,144,1024]{3,2,0,1:T(8,128)(2,1)S(1)}, u32[]{:S(2)}, u32[]{:S(2)}) collective-permute-start(bf16[2,1,144,1024]{3,2,0,1:T(8,128)(2,1)S(1)} %bitcast.152), channel_id=1, source_target_pairs={{0,16},{2,18},{4,20},{6,22},{8,24},{10,26},{12,28},{14,30},{16,0},... | collective-permute-start | bytes 1769480 | tf_op jit(solution)/shard_map/ppermute | solution.py:221
  163.8 103.2 %collective-permute-start.1 = (bf16[2,1,144,1024]{3,2,0,1:T(8,128)(2,1)S(1)}, bf16[2,1,144,1024]{3,2,0,1:T(8,128)(2,1)S(1)}, u32[]{:S(2)}, u32[]{:S(2)}) collective-permute-start(bf16[2,1,144,1024]{3,2,0,1:T(8,128)(2,1)S(1)} %bitcast.153), channel_id=1, source_target_pairs={{0,24},{2,26},{4,28},{6,30},{8,16},{10,18},{12,20},{14,22},{16,8},... | collective-permute-start | bytes 1769480 | tf_op jit(solution)/shard_map/ppermute | solution.py:221
  165.1 59.7 %copy-start.10 = (bf16[64,1,128,128]{3,2,1,0:T(8,128)(2,1)S(1)}, bf16[64,1,128,128]{3,2,1,0:T(8,128)(2,1)}, u32[]{:S(2)}) copy-start(bf16[64,1,128,128]{3,2,1,0:T(8,128)(2,1)} %get-tuple-element.44.k_ref) | copy-start | bytes 6291460
  171.0 59.9 %copy-start.13 = (f32[2,1,144,1024]{3,2,1,0:T(8,128)}, f32[2,1,144,1024]{3,2,1,0:T(8,128)S(1)}, u32[]{:S(2)}) copy-start(f32[2,1,144,1024]{3,2,1,0:T(8,128)S(1)} %shard_map.81) | copy-start | bytes 3538948
  224.8 6.1 %copy-start.15 = (bf16[2,1,144,1024]{3,2,0,1:T(8,128)(2,1)}, bf16[2,1,144,1024]{3,2,0,1:T(8,128)(2,1)S(1)}, u32[]{:S(2)}) copy-start(bf16[2,1,144,1024]{3,2,0,1:T(8,128)(2,1)S(1)} %collective-permute-done.2) | copy-start | bytes 1769476
  230.9 68.3 %collective-permute-start.6 = (bf16[2,1,144,1024]{3,2,1,0:T(8,128)(2,1)}, bf16[2,1,144,1024]{3,2,1,0:T(8,128)(2,1)}, u32[]{:S(2)}, u32[]{:S(2)}) collective-permute-start(bf16[2,1,144,1024]{3,2,1,0:T(8,128)(2,1)} %shard_map.80), channel_id=1, source_target_pairs={{0,4},{2,6},{4,0},{6,2},{8,12},{10,14},{12,8},{14,10},{16,20},{18,... | collective-permute-start | bytes 1769480 | tf_op jit(solution)/shard_map/ppermute | solution.py:221
  230.9 6.1 %copy-start.17 = (bf16[2,1,144,1024]{3,2,0,1:T(8,128)(2,1)}, bf16[2,1,144,1024]{3,2,0,1:T(8,128)(2,1)S(1)}, u32[]{:S(2)}) copy-start(bf16[2,1,144,1024]{3,2,0,1:T(8,128)(2,1)S(1)} %collective-permute-done) | copy-start | bytes 1769476
  237.0 68.7 %collective-permute-start.4 = (bf16[2,1,144,1024]{3,2,0,1:T(8,128)(2,1)}, bf16[2,1,144,1024]{3,2,0,1:T(8,128)(2,1)}, u32[]{:S(2)}, u32[]{:S(2)}) collective-permute-start(bf16[2,1,144,1024]{3,2,0,1:T(8,128)(2,1)} %bitcast.41), channel_id=1, source_target_pairs={{0,12},{2,14},{4,8},{6,10},{8,4},{10,6},{12,0},{14,2},{16,28},{18,... | collective-permute-start | bytes 1769480 | tf_op jit(solution)/shard_map/ppermute | solution.py:221
  266.2 0.8 copy-start.19
  267.0 7.0 %copy-start.22 = (bf16[2,1,144,1024]{3,2,0,1:T(8,128)(2,1)}, bf16[2,1,144,1024]{3,2,0,1:T(8,128)(2,1)S(1)}, u32[]{:S(2)}) copy-start(bf16[2,1,144,1024]{3,2,0,1:T(8,128)(2,1)S(1)} %collective-permute-done.1) | copy-start | bytes 1769476
  274.0 32.5 %collective-permute-start.5 = (bf16[2,1,144,1024]{3,2,0,1:T(8,128)(2,1)}, bf16[2,1,144,1024]{3,2,0,1:T(8,128)(2,1)}, u32[]{:S(2)}, u32[]{:S(2)}) collective-permute-start(bf16[2,1,144,1024]{3,2,0,1:T(8,128)(2,1)} %bitcast.44), channel_id=1, source_target_pairs={{0,8},{2,10},{4,12},{6,14},{8,0},{10,2},{12,4},{14,6},{16,24},{18,... | collective-permute-start | bytes 1769480 | tf_op jit(solution)/shard_map/ppermute | solution.py:221
  285.9 2.2 copy-start.2
  288.1 1.6 copy-start.5
  289.7 1.1 copy-start.20
  290.8 8.3 %copy-start.18 = (bf16[2,1,144,1024]{3,2,0,1:T(8,128)(2,1)S(1)}, bf16[2,1,144,1024]{3,2,0,1:T(8,128)(2,1)}, u32[]{:S(2)}) copy-start(bf16[2,1,144,1024]{3,2,0,1:T(8,128)(2,1)} %copy-done.17) | copy-start | bytes 1769476
  290.8 8.3 %copy-start.23 = (bf16[2,1,144,1024]{3,2,0,1:T(8,128)(2,1)S(1)}, bf16[2,1,144,1024]{3,2,0,1:T(8,128)(2,1)}, u32[]{:S(2)}) copy-start(bf16[2,1,144,1024]{3,2,0,1:T(8,128)(2,1)} %copy-done.22) | copy-start | bytes 1769476
  296.2 19.1 %collective-permute-start.7 = (bf16[2,1,144,1024]{3,2,0,1:T(8,128)(2,1)S(1)}, bf16[2,1,144,1024]{3,2,0,1:T(8,128)(2,1)S(1)}, u32[]{:S(2)}, u32[]{:S(2)}) collective-permute-start(bf16[2,1,144,1024]{3,2,0,1:T(8,128)(2,1)S(1)} %bitcast.161), channel_id=1, source_target_pairs={{0,28},{2,30},{4,24},{6,26},{8,20},{10,22},{12,16},{14,18},{16,12}... | collective-permute-start | bytes 1769480 | tf_op jit(solution)/shard_map/ppermute | solution.py:221
  304.8 106.7 %collective-permute-start.10 = (bf16[2,1,144,1024]{3,2,0,1:T(8,128)(2,1)S(1)}, bf16[2,1,144,1024]{3,2,0,1:T(8,128)(2,1)S(1)}, u32[]{:S(2)}, u32[]{:S(2)}) collective-permute-start(bf16[2,1,144,1024]{3,2,0,1:T(8,128)(2,1)S(1)} %bitcast.156), channel_id=1, source_target_pairs={{0,16},{2,18},{4,20},{6,22},{8,24},{10,26},{12,28},{14,30},{16,0},... | collective-permute-start | bytes 1769480 | tf_op jit(solution)/shard_map/ppermute | solution.py:221
  315.3 33.0 %copy-start.3 = (bf16[16,1,128,1024]{3,2,1,0:T(8,128)(2,1)S(1)}, bf16[16,1,128,1024]{3,2,1,0:T(8,128)(2,1)}, u32[]{:S(2)}) copy-start(bf16[16,1,128,1024]{3,2,1,0:T(8,128)(2,1)} %all-gather.6.cloned.1.call-done.q_ref) | copy-start | bytes 12582916
  320.7 90.8 %collective-permute-start.11 = (bf16[2,1,144,1024]{3,2,0,1:T(8,128)(2,1)S(1)}, bf16[2,1,144,1024]{3,2,0,1:T(8,128)(2,1)S(1)}, u32[]{:S(2)}, u32[]{:S(2)}) collective-permute-start(bf16[2,1,144,1024]{3,2,0,1:T(8,128)(2,1)S(1)} %bitcast.157), channel_id=1, source_target_pairs={{0,12},{2,14},{4,8},{6,10},{8,4},{10,6},{12,0},{14,2},{16,28},{18,... | collective-permute-start | bytes 1769480 | tf_op jit(solution)/shard_map/ppermute | solution.py:221
  354.7 20.1 %collective-permute-start.8 = (bf16[2,1,144,1024]{3,2,0,1:T(8,128)(2,1)S(1)}, bf16[2,1,144,1024]{3,2,0,1:T(8,128)(2,1)S(1)}, u32[]{:S(2)}, u32[]{:S(2)}) collective-permute-start(bf16[2,1,144,1024]{3,2,0,1:T(8,128)(2,1)S(1)} %bitcast.158), channel_id=1, source_target_pairs={{0,24},{2,26},{4,28},{6,30},{8,16},{10,18},{12,20},{14,22},{16,8},... | collective-permute-start | bytes 1769480 | tf_op jit(solution)/shard_map/ppermute | solution.py:221
  354.7 5.7 %copy-start.16 = (bf16[2,1,144,1024]{3,2,0,1:T(8,128)(2,1)S(1)}, bf16[2,1,144,1024]{3,2,0,1:T(8,128)(2,1)}, u32[]{:S(2)}) copy-start(bf16[2,1,144,1024]{3,2,0,1:T(8,128)(2,1)} %copy-done.15) | copy-start | bytes 1769476
  354.8 5.7 %copy-start.21 = (bf16[2,1,144,1024]{3,2,0,1:T(8,128)(2,1)S(1)}, bf16[2,1,144,1024]{3,2,0,1:T(8,128)(2,1)}, u32[]{:S(2)}) copy-start(bf16[2,1,144,1024]{3,2,0,1:T(8,128)(2,1)} %copy-done.19) | copy-start | bytes 1769476
  360.2 45.5 %collective-permute-start.9 = (bf16[2,1,144,1024]{3,2,1,0:T(8,128)(2,1)S(1)}, bf16[2,1,144,1024]{3,2,1,0:T(8,128)(2,1)S(1)}, u32[]{:S(2)}, u32[]{:S(2)}) collective-permute-start(bf16[2,1,144,1024]{3,2,1,0:T(8,128)(2,1)S(1)} %shard_map.84), channel_id=1, source_target_pairs={{0,20},{2,22},{4,16},{6,18},{8,28},{10,30},{12,24},{14,26},{16,4},... | collective-permute-start | bytes 1769480 | tf_op jit(solution)/shard_map/ppermute | solution.py:221
  381.1 34.2 %collective-permute-start.12 = (bf16[2,1,144,1024]{3,2,0,1:T(8,128)(2,1)S(1)}, bf16[2,1,144,1024]{3,2,0,1:T(8,128)(2,1)S(1)}, u32[]{:S(2)}, u32[]{:S(2)}) collective-permute-start(bf16[2,1,144,1024]{3,2,0,1:T(8,128)(2,1)S(1)} %bitcast.159), channel_id=1, source_target_pairs={{0,8},{2,10},{4,12},{6,14},{8,0},{10,2},{12,4},{14,6},{16,24},{18,... | collective-permute-start | bytes 1769480 | tf_op jit(solution)/shard_map/ppermute | solution.py:221
  411.2 13.0 %copy-start.14 = (f32[2,1,144,1024]{3,2,1,0:T(8,128)S(1)}, f32[2,1,144,1024]{3,2,1,0:T(8,128)}, u32[]{:S(2)}) copy-start(f32[2,1,144,1024]{3,2,1,0:T(8,128)} %copy-done.13) | copy-start | bytes 3538948
  411.2 12.8 %collective-permute-start.13 = (bf16[2,1,144,1024]{3,2,0,1:T(8,128)(2,1)S(1)}, bf16[2,1,144,1024]{3,2,0,1:T(8,128)(2,1)S(1)}, u32[]{:S(2)}, u32[]{:S(2)}) collective-permute-start(bf16[2,1,144,1024]{3,2,0,1:T(8,128)(2,1)S(1)} %bitcast.160), channel_id=1, source_target_pairs={{0,4},{2,6},{4,0},{6,2},{8,12},{10,14},{12,8},{14,10},{16,20},{18,... | collective-permute-start | bytes 1769480 | tf_op jit(solution)/shard_map/ppermute | solution.py:221
Sparse Core Ops, SparseCore 0:
  40.3 73.9 all-gather.3
  116.4 138.7 all-gather.5
